TPU v7x, 128 devices: a whole 4x4x4 slice. The times are simulated.
128 devices in a mesh: tm: 4 (over y_lo, core), height: 32 (over y_hi, z, x).
Axes of the slice: x: 4, y: 4 (y_hi: 2, y_lo: 2; y = y_hi * 2 + y_lo), z: 4, core: 2. Of those that a mesh axis runs over, the one named last changes fastest.
Arguments:
- latents: bfloat16 [8, 64, 640, 384], P('tm', 'height'), may hold values from -6 to 6
- cotangent: bfloat16 [8, 64, 640, 384], P('tm', 'height'), may hold values from -6 to 6
- temporal_weight: bfloat16 [3, 384, 384], replicated, may hold values from -0.1875 to 0.1875
- spatial_weight: bfloat16 [3, 3, 384, 384], replicated, may hold values from -0.109375 to 0.109375
Outputs:
- latent_grad: bfloat16 [8, 64, 640, 384], P('tm', 'height')
- temporal_grad: float32 [3, 384, 384], replicated
- spatial_grad: float32 [3, 3, 384, 384], replicated
All inputs are finite; a program needn't handle non-finite values.
Results may differ from a plain program's by a relative error of at most 0.0054.
Values may be sent and summed in bfloat16 or wider, within the bound.
A program may use at most 128 MiB of HBM per device.

v0:
```python
import math

import jax
import jax.numpy as jnp
from jax import lax
from jax.sharding import PartitionSpec as P


def shifted(array, axis, by):
    size = lax.axis_size(axis)
    pairs = [(i, i + by) for i in range(size) if 0 <= i + by < size]
    return lax.ppermute(array, axis, pairs)


def extended(array, sides, width):
    for axis, dim in sides:
        size, length = (lax.axis_size(axis), array.shape[dim])
        up = [(i, (i + 1) % size) for i in range(size - 1)]
        down = [(j, i) for i, j in up]
        last = lax.slice_in_dim(array, length - width, length, axis=dim)
        first = lax.slice_in_dim(array, 0, width, axis=dim)
        before = lax.ppermute(last, axis, up)
        after = lax.ppermute(first, axis, down)
        array = jnp.concatenate([before, array, after], axis=dim)
    return array


def flat(value):
    return value.reshape(-1, value.shape[-1])


def inner(left, right):
    return lax.dot_general(
        left, right, (((0,), (0,)), ((), ())), preferred_element_type=jnp.float32
    )


def backward(left, weight):
    return lax.dot_general(
        left, weight, (((1,), (1,)), ((), ())), preferred_element_type=jnp.float32
    )


def on_device(latents, cotangent, temporal_weight, spatial_weight):
    frames, rows, cols, chans = latents.shape
    count = frames * lax.axis_size("tm") * rows * lax.axis_size("height") * cols
    scale = 1.0 / math.sqrt(count)
    earlier = shifted(latents, "tm", 1)
    before = jnp.concatenate([earlier, latents], axis=0)
    pre = jnp.zeros((frames * rows * cols, chans), jnp.float32)
    for tap in range(3):
        pre = pre + jnp.dot(
            flat(before[2 - tap : 2 - tap + frames]),
            temporal_weight[tap],
            preferred_element_type=jnp.float32,
        )
    hidden = jax.nn.silu(pre).astype(jnp.bfloat16)
    rimmed = extended(cotangent, (("height", 1),), 1)
    padded = jnp.pad(rimmed, ((0, 0), (0, 0), (1, 1), (0, 0)))
    back = jnp.zeros((frames * rows * cols, chans), jnp.float32)
    spatial = []
    for i in range(3):
        for j in range(3):
            window = flat(padded[:, 2 - i : 2 - i + rows, 2 - j : 2 - j + cols])
            back = back + backward(window, spatial_weight[i, j])
            spatial.append(inner(hidden, window))
    sigma = jax.nn.sigmoid(pre)
    pre_grad = (back * sigma * (1.0 + pre * (1.0 - sigma))).astype(jnp.bfloat16)
    grid = pre_grad.reshape(frames, rows, cols, chans)
    temporal = []
    for tap in range(3):
        temporal.append(inner(flat(before[2 - tap : 2 - tap + frames]), pre_grad))
    total = flat(cotangent).astype(jnp.float32)
    later = shifted(grid, "tm", -1)
    after = jnp.concatenate([grid, later], axis=0)
    for tap in range(3):
        total = total + backward(flat(after[tap : tap + frames]), temporal_weight[tap])
    latent_grad = total.reshape(frames, rows, cols, chans).astype(jnp.bfloat16)
    temporal_local = jnp.stack(temporal)
    spatial_local = jnp.stack(spatial).reshape(3, 3, chans, chans)
    temporal_sum, spatial_sum = lax.psum((temporal_local, spatial_local), ("tm", "height"))
    return (latent_grad, temporal_sum * scale, spatial_sum * scale)


def solution(mesh):
    return jax.shard_map(
        on_device,
        mesh=mesh,
        in_specs=(P("tm", "height", None, None), P("tm", "height", None, None), P(), P()),
        out_specs=(P("tm", "height", None, None), P(), P()),
        check_vma=False,
    )
```

profile of v0, /device:TPU:1, one launch (start us, length us, event | category | flops | bytes accessed | tf_op | source)
XLA Modules:
  0.0 284.4 jit_solution(17161190621153007249)
XLA Ops:
  7.2 0.0 all-reduce.4.cloned.1.call-start
  7.2 1.8 fusion.56
  9.0 1.3 collective-permute-start.1
  10.3 4.6 %collective-permute-start = (bf16[2,1,640,384]{3,2,1,0:T(8,128)(2,1)S(1)}, bf16[2,1,640,384]{3,2,1,0:T(8,128)(2,1)S(1)}, u32[]{:S(2)}, u32[]{:S(2)}) collective-permute-start(bf16[2,1,640,384]{3,2,1,0:T(8,128)(2,1)S(1)} %get-tuple-element.16), channel_id=1, source_target_pairs={{0,1},{1,2},{2,3},{3,4},{4,5},{5,6},{6,7},{7,8},{8,9},{9,10},{10,1... | collective-permute-start | bytes 2949128 | tf_op jit(solution)/shard_map/ppermute | solution.py:22
  14.9 4.6 %collective-permute-start.2 = (bf16[2,2,640,384]{3,2,1,0:T(8,128)(2,1)}, bf16[2,2,640,384]{3,2,1,0:T(8,128)(2,1)}, u32[]{:S(2)}, u32[]{:S(2)}) collective-permute-start(bf16[2,2,640,384]{3,2,1,0:T(8,128)(2,1)} %param.4), channel_id=1, source_target_pairs={{0,32},{32,64},{64,96},{1,33},{33,65},{65,97},{2,34},{34,66},{66,9... | collective-permute-start | bytes 5898248 | tf_op jit(solution)/shard_map/ppermute | solution.py:12
  19.5 3.0 %fusion.27 = f32[2560,384]{1,0:T(8,128)S(1)} fusion(bf16[2560,384]{1,0:T(8,128)(2,1)} %bitcast.18, bf16[3,384,384]{2,1,0:T(8,128)(2,1)S(1)} %copy-done.5), kind=kOutput, calls=%fused_computation.61 | convolution fusion | flops 754974720 | bytes 6193152 | tf_op jit(solution)/shard_map/dot_general | solution.py:52
  22.6 11.3 %collective-permute-done.1 = bf16[2,1,640,384]{3,2,1,0:T(8,128)(2,1)S(1)} collective-permute-done((bf16[2,1,640,384]{3,2,1,0:T(8,128)(2,1)S(1)}, bf16[2,1,640,384]{3,2,1,0:T(8,128)(2,1)S(1)}, u32[]{:S(2)}, u32[]{:S(2)}) %collective-permute-start.1) | collective-permute-done | bytes 983072 | tf_op jit(solution)/shard_map/ppermute | solution.py:23
  33.9 0.9 collective-permute-done
  34.8 1.3 fusion.11
  36.1 2.4 fusion.55
  38.5 2.3 fusion.38
  40.9 1.7 pad_maximum_fusion.2
  42.6 2.4 convolution_add_fusion.10
  45.0 2.5 convolution_add_fusion.9
  47.5 2.3 fusion.29
  49.8 2.4 convolution_add_fusion.8
  52.2 2.4 convolution_add_fusion.7
  54.6 2.4 convolution_add_fusion.6
  57.0 4.4 %convolution_add_fusion.5 = f32[2560,384]{1,0:T(8,128)} fusion(f32[2560,384]{1,0:T(8,128)S(1)} %convolution_add_fusion.6, bf16[2560,384]{1,0:T(8,128)(2,1)S(1)} %bitcast.158, bf16[3,3,384,384]{3,2,1,0:T(8,128)(2,1)} %param.7), kind=kOutput, calls=%fused_computation.15 | convolution fusion | flops 755957760 | bytes 10125312 | tf_op jit(solution)/shard_map/dot_general | solution.py:39
  61.4 1.7 pad_maximum_fusion.1
  63.1 1.5 convolution_add_fusion.3
  64.6 6.2 %multiply_convert_fusion = (bf16[2560,384]{1,0:T(8,128)(2,1)}, f32[2560,384]{1,0:T(8,128)}) fusion(f32[2560,384]{1,0:T(8,128)S(1)} %convolution_add_fusion.3, bf16[2560,384]{1,0:T(8,128)(2,1)} %bitcast.22, bf16[3,384,384]{2,1,0:T(8,128)(2,1)S(1)} %copy-done.5), kind=kOutput, calls=%fused_computation.25 | convolution fusion | flops 760872960 | bytes 12091392 | tf_op jit(solution)/shard_map/dot_general | solution.py:52
  70.8 4.3 %fusion.8 = bf16[2560,384]{1,0:T(8,128)(2,1)S(1)} fusion(f32[2560,384]{1,0:T(8,128)S(1)} %fusion.29, f32[2560,384]{1,0:T(8,128)S(1)} %copy-done.4, bf16[2560,384]{1,0:T(8,128)(2,1)S(1)} %bitcast.171, f32[2560,384]{1,0:T(8,128)} %get-tuple-element.19, bf16[3,3,384,384]{3,2,1,0:T(8,128)(2,1)} %param.7), kind=kOutput, calls=%fused_computation.21 | convolution fusion | flops 765788160 | bytes 16023552 | tf_op jit(solution)/shard_map/dot_general | solution.py:39
  75.1 3.5 %convolution_bitcast_fusion.9 = f32[1,384,384]{1,2,0:T(8,128)S(1)} fusion(bf16[2560,384]{1,0:T(8,128)(2,1)S(1)} %fusion.8, bf16[2560,384]{1,0:T(8,128)(2,1)} %bitcast.22), kind=kOutput, calls=%fused_computation.51 | convolution fusion | flops 754974720 | bytes 4521984 | tf_op jit(solution)/shard_map/dot_general | solution.py:33
  78.5 1.2 convolution_bitcast_fusion.10
  79.8 2.9 %convolution_bitcast_fusion.11 = f32[1,384,384]{1,2,0:T(8,128)S(1)} fusion(bf16[2560,384]{1,0:T(8,128)(2,1)S(1)} %fusion.8, bf16[2560,384]{1,0:T(8,128)(2,1)} %bitcast.18), kind=kOutput, calls=%fused_computation.53 | convolution fusion | flops 754974720 | bytes 4521984 | tf_op jit(solution)/shard_map/dot_general | solution.py:33
  82.7 1.2 fusion.20
  83.9 1.2 fusion.19
  85.1 1.2 fusion.18
  86.3 1.2 fusion.17
  87.5 1.2 fusion.16
  88.7 1.2 fusion.15
  89.9 1.2 fusion.14
  91.1 1.2 fusion.13
  92.3 1.2 fusion.12
  93.6 2.4 copy-done.3
  95.9 1.3 pad_maximum_fusion.4
  97.2 0.0 all-reduce.4.cloned.1.call-update
  97.3 4.3 %collective-permute-start.3 = (bf16[2,2,640,384]{3,2,1,0:T(8,128)(2,1)}, bf16[2,2,640,384]{3,2,1,0:T(8,128)(2,1)S(1)}, u32[]{:S(2)}, u32[]{:S(2)}) collective-permute-start(bf16[2,2,640,384]{3,2,1,0:T(8,128)(2,1)} %bitcast.151), channel_id=1, source_target_pairs={{32,0},{64,32},{96,64},{33,1},{65,33},{97,65},{34,2},{66,34},{98,6... | collective-permute-start | bytes 5898248 | tf_op jit(solution)/shard_map/ppermute | solution.py:12
  101.6 2.9 %convolution_add_fusion.1 = f32[2560,384]{1,0:T(8,128)S(1)} fusion(bf16[2560,384]{1,0:T(8,128)(2,1)} %copy-done.1, bf16[2560,384]{1,0:T(8,128)(2,1)S(1)} %bitcast.148, bf16[3,384,384]{2,1,0:T(8,128)(2,1)S(1)} %copy-done.5), kind=kOutput, calls=%fused_computation.8 | convolution fusion | flops 756940800 | bytes 8159232 | tf_op jit(solution)/shard_map/dot_general | solution.py:39
  104.5 25.4 %collective-permute-done.3 = bf16[2,2,640,384]{3,2,1,0:T(8,128)(2,1)S(1)} collective-permute-done((bf16[2,2,640,384]{3,2,1,0:T(8,128)(2,1)}, bf16[2,2,640,384]{3,2,1,0:T(8,128)(2,1)S(1)}, u32[]{:S(2)}, u32[]{:S(2)}) %collective-permute-start.3) | collective-permute-done | bytes 1966112 | tf_op jit(solution)/shard_map/ppermute | solution.py:12
  130.0 0.2 pad_maximum_fusion
  130.2 1.4 fusion.21
  131.6 2.7 fusion.9
  134.3 134.6 %all-reduce.4.cloned.1.call-done = (f32[3,384,384]{1,2,0:T(8,128)}, f32[3,3,384,384]{3,2,1,0:T(8,128)}) async-done(((f32[3,384,384]{1,2,0:T(8,128)}, f32[3,3,384,384]{3,2,1,0:T(8,128)}), (f32[3,384,384]{1,2,0:T(8,128)}, f32[3,3,384,384]{3,2,1,0:T(8,128)})) %all-reduce.4.cloned.1.call-update) | async-done | bytes 7077904 | tf_op jit(solution)/shard_map/psum | solution.py:81
  268.8 1.6 broadcast_multiply_fusion.1
  270.4 1.8 copy.8
  272.3 5.3 %broadcast_multiply_fusion = f32[3,3,384,384]{3,2,1,0:T(8,128)} fusion(f32[3,3,384,384]{3,2,1,0:T(8,128)} %get-tuple-element.7), kind=kLoop, calls=%fused_computation.27 | loop fusion | flops 1327104 | bytes 10616832 | tf_op jit(solution)/shard_map/mul | solution.py:82
  (16 shorter events, 0.0 us)
Async XLA Ops:
  7.2 12.4 %copy-start.5 = (bf16[3,384,384]{2,1,0:T(8,128)(2,1)S(1)}, bf16[3,384,384]{2,1,0:T(8,128)(2,1)}, u32[]{:S(2)}) copy-start(bf16[3,384,384]{2,1,0:T(8,128)(2,1)} %param.6) | copy-start | bytes 2654212
  7.2 261.6 %all-reduce.4.cloned.1.call-start = ((), (), s32[]{:S(2)}) async-start(), calls=%async_computation | async-start | bytes 14155776 | tf_op jit(solution)/shard_map/psum | solution.py:81
  9.0 24.9 %collective-permute-start.1 = (bf16[2,1,640,384]{3,2,1,0:T(8,128)(2,1)S(1)}, bf16[2,1,640,384]{3,2,1,0:T(8,128)(2,1)S(1)}, u32[]{:S(2)}, u32[]{:S(2)}) collective-permute-start(bf16[2,1,640,384]{3,2,1,0:T(8,128)(2,1)S(1)} %get-tuple-element.17), channel_id=1, source_target_pairs={{1,0},{2,1},{3,2},{4,3},{5,4},{6,5},{7,6},{8,7},{9,8},{10,9},{11,1... | collective-permute-start | bytes 2949128 | tf_op jit(solution)/shard_map/ppermute | solution.py:23
  10.3 24.5 %collective-permute-start = (bf16[2,1,640,384]{3,2,1,0:T(8,128)(2,1)S(1)}, bf16[2,1,640,384]{3,2,1,0:T(8,128)(2,1)S(1)}, u32[]{:S(2)}, u32[]{:S(2)}) collective-permute-start(bf16[2,1,640,384]{3,2,1,0:T(8,128)(2,1)S(1)} %get-tuple-element.16), channel_id=1, source_target_pairs={{0,1},{1,2},{2,3},{3,4},{4,5},{5,6},{6,7},{7,8},{8,9},{9,10},{10,1... | collective-permute-start | bytes 2949128 | tf_op jit(solution)/shard_map/ppermute | solution.py:22
  14.9 46.5 %collective-permute-start.2 = (bf16[2,2,640,384]{3,2,1,0:T(8,128)(2,1)}, bf16[2,2,640,384]{3,2,1,0:T(8,128)(2,1)}, u32[]{:S(2)}, u32[]{:S(2)}) collective-permute-start(bf16[2,2,640,384]{3,2,1,0:T(8,128)(2,1)} %param.4), channel_id=1, source_target_pairs={{0,32},{32,64},{64,96},{1,33},{33,65},{65,97},{2,34},{34,66},{66,9... | collective-permute-start | bytes 5898248 | tf_op jit(solution)/shard_map/ppermute | solution.py:12
  19.5 15.3 %copy-start = (bf16[2,2,640,384]{3,2,1,0:T(8,128)(2,1)S(1)}, bf16[2,2,640,384]{3,2,1,0:T(8,128)(2,1)}, u32[]{:S(2)}) copy-start(bf16[2,2,640,384]{3,2,1,0:T(8,128)(2,1)} %param.5) | copy-start | bytes 5898244
  64.6 6.2 %copy-start.4 = (f32[2560,384]{1,0:T(8,128)S(1)}, f32[2560,384]{1,0:T(8,128)}, u32[]{:S(2)}) copy-start(f32[2560,384]{1,0:T(8,128)} %convolution_add_fusion.5) | copy-start | bytes 11796484
  64.6 6.2 %copy-start.6 = (bf16[2,2,640,384]{3,2,1,0:T(8,128)(2,1)S(1)}, bf16[2,2,640,384]{3,2,1,0:T(8,128)(2,1)}, u32[]{:S(2)}) copy-start(bf16[2,2,640,384]{3,2,1,0:T(8,128)(2,1)} %get-tuple-element.14) | copy-start | bytes 5898244
  75.1 7.6 %copy-start.1 = (bf16[2560,384]{1,0:T(8,128)(2,1)}, bf16[2560,384]{1,0:T(8,128)(2,1)S(1)}, u32[]{:S(2)}) copy-start(bf16[2560,384]{1,0:T(8,128)(2,1)S(1)} %fusion.8) | copy-start | bytes 5898244
  79.8 2.9 %copy-start.7 = (bf16[2560,384]{1,0:T(8,128)(2,1)S(1)}, bf16[2560,384]{1,0:T(8,128)(2,1)}, u32[]{:S(2)}) copy-start(bf16[2560,384]{1,0:T(8,128)(2,1)} %get-tuple-element.18) | copy-start | bytes 5898244
  93.5 2.4 copy-start.3
  97.3 32.7 %copy-start.2 = (bf16[2560,384]{1,0:T(8,128)(2,1)S(1)}, bf16[2560,384]{1,0:T(8,128)(2,1)}, u32[]{:S(2)}) copy-start(bf16[2560,384]{1,0:T(8,128)(2,1)} %copy-done.1) | copy-start | bytes 5898244
  97.3 32.7 %collective-permute-start.3 = (bf16[2,2,640,384]{3,2,1,0:T(8,128)(2,1)}, bf16[2,2,640,384]{3,2,1,0:T(8,128)(2,1)S(1)}, u32[]{:S(2)}, u32[]{:S(2)}) collective-permute-start(bf16[2,2,640,384]{3,2,1,0:T(8,128)(2,1)} %bitcast.151), channel_id=1, source_target_pairs={{32,0},{64,32},{96,64},{33,1},{65,33},{97,65},{34,2},{66,34},{98,6... | collective-permute-start | bytes 5898248 | tf_op jit(solution)/shard_map/ppermute | solution.py:12
Sparse Core Ops, SparseCore 0:
  97.4 171.3 all-reduce.3
where the time goes:
time: 285 us; the launch traced here: 284 us
  waiting for transfers between devices  172 us (60%)
  matrix products  61.3 us (22%)
  starting transfers between devices  14.9 us (5%)
  between operations  14.4 us (5%)
  other arithmetic  13.2 us (5%)
  local copies, waits for them, and re-layouts  8.44 us (3%)
    psum x1, waiting for transfers between devices, on_device(): lax.psum((temporal_local, spatial_local), ('tm', 'height'))  135 us
    dot_general x12, matrix products, backward(): lax.dot_general(left, weight, (((1,), (1,)), ((), ())), preferred_element...  32.3 us
    ppermute x2, waiting for transfers between devices, shifted(): return lax.ppermute(array, axis, pairs)  25.5 us
    dot_general x12, matrix products, inner(): lax.dot_general(left, right, (((0,), (0,)), ((), ())), preferred_element_...  18.4 us
    ppermute x1, waiting for transfers between devices, extended(): after = lax.ppermute(first, axis, down)  11.3 us
    dot_general x3, matrix products, on_device(): jnp.dot(flat(before[2 - tap:2 - tap + frames]), temporal_weight[tap], pre...  10.7 us
    ppermute x2, starting transfers between devices, shifted(): return lax.ppermute(array, axis, pairs)  8.91 us
    mul x2, other arithmetic, on_device(): return (latent_grad, temporal_sum * scale, spatial_sum * scale)  6.97 us
  transfers between devices with their start and end apart: 5, of which 4 were waited for; matrix products, arithmetic and copies ran while one was open for 13% of the time, Pallas kernels for 0%

commit v1 on v0

--- a/solution.py
+++ b/solution.py
@@ -3,7 +3,270 @@
 import jax
 import jax.numpy as jnp
 from jax import lax
+from jax.experimental import pallas as pl
+from jax.experimental.pallas import tpu as pltpu
 from jax.sharding import PartitionSpec as P
+
+BF = jnp.bfloat16
+F32 = jnp.float32
+MESH = pl.DeviceIdType.MESH
+HALF = 192
+QUART = 48
+
+
+class Place:
+    def __init__(self):
+        tm = lax.axis_index("tm")
+        height = lax.axis_index("height")
+        self.tm = tm
+        self.height = height
+        self.core = tm % 2
+        self.xyz = (height % 4, (height // 16) * 2 + tm // 2, (height // 4) % 4)
+
+    def at(self, x, y, z, core):
+        return ((y % 2) * 2 + core, (y // 2) * 16 + z * 4 + x)
+
+    def along(self, axis, where):
+        xyz = list(self.xyz)
+        xyz[axis] = where
+        return self.at(*xyz, self.core)
+
+    def other(self):
+        return (self.tm + 1 - 2 * self.core, self.height)
+
+
+def remote(src, dst, send, recv, device):
+    return pltpu.make_async_remote_copy(
+        src_ref=src, dst_ref=dst, send_sem=send, recv_sem=recv,
+        device_id=device, device_id_type=MESH)
+
+
+class Reduce:
+    SCRATCH = [
+        pltpu.VMEM((12, HALF, 384), BF),
+        pltpu.VMEM((12, HALF, 384), BF),
+        pltpu.VMEM((12, HALF, 384), BF),
+        pltpu.VMEM((12, QUART, 384), F32),
+        pltpu.VMEM((12, 3, QUART, 384), BF),
+        pltpu.VMEM((12, QUART, 384), BF),
+        pltpu.VMEM((3, 3, QUART, 384), BF),
+        pltpu.VMEM((3, 4, QUART, 384), BF),
+        pltpu.SemaphoreType.DMA((12, 2)),
+        pltpu.SemaphoreType.DMA((12, 3, 2)),
+        pltpu.SemaphoreType.DMA((12,)),
+        pltpu.SemaphoreType.DMA((3, 3)),
+        pltpu.SemaphoreType.DMA((3, 3, 2)),
+        pltpu.SemaphoreType.DMA((3, 3)),
+        pltpu.SemaphoreType.DMA((12,)),
+        pltpu.SemaphoreType.DMA((12, 3, 2)),
+        pltpu.SemaphoreType.DMA((12, 2)),
+    ]
+
+    def __init__(self, place, part, out, refs):
+        self.place = place
+        self.part = part
+        self.out = out
+        (self.c_out, self.c_in, self.q_out, self.q_own, self.q_in, self.s_out, self.s_in, self.t_buf,
+         self.c_sem, self.q_sem, self.s_send, self.s_recv, self.t_sem, self.g2_send, self.g2_recv,
+         self.g1_sem, self.gc_sem) = refs
+
+    def core_copy(self, t):
+        return remote(self.c_out.at[t], self.c_in.at[t], self.c_sem.at[t, 0], self.c_sem.at[t, 1], self.place.other())
+
+    def quarter_copy(self, t, o, d):
+        q = (self.place.xyz[o] + d) % 4
+        return remote(self.q_out.at[t, pl.ds(q * QUART, QUART)], self.q_in.at[t, d - 1],
+                      self.q_sem.at[t, d - 1, 0], self.q_sem.at[t, d - 1, 1], self.place.along(o, q))
+
+    def second_copy(self, t, o, g, slot):
+        b = (o + 1) % 3
+        return remote(self.s_out.at[t], self.s_in.at[o, slot], self.s_send.at[t], self.s_recv.at[o, slot],
+                      self.place.along(b, g))
+
+    def third_copy(self, o, d):
+        b = (o + 2) % 3
+        p = self.place.xyz[b]
+        return remote(self.t_buf.at[o, p], self.t_buf.at[o, p], self.t_sem.at[o, d - 1, 0], self.t_sem.at[o, d - 1, 1],
+                      self.place.along(b, (p + d) % 4))
+
+    def third_wait(self, o, d):
+        p = (self.place.xyz[(o + 2) % 3] + 4 - d) % 4
+        return remote(self.t_buf.at[o, p], self.t_buf.at[o, p], self.t_sem.at[o, d - 1, 0], self.t_sem.at[o, d - 1, 1],
+                      self.place.other())
+
+    def rows(self, t, q):
+        return self.out.at[t, pl.ds(self.place.core * HALF + q * QUART, QUART)]
+
+    def gather2_copy(self, t, o, d):
+        b = (o + 1) % 3
+        ref = self.rows(t, self.place.xyz[o])
+        return remote(ref, ref, self.g2_send.at[o, d - 1], self.g2_recv.at[t],
+                      self.place.along(b, (self.place.xyz[b] + d) % 4))
+
+    def gather1_copy(self, t, o, d):
+        p = self.place.xyz[o]
+        ref = self.rows(t, p)
+        return remote(ref, ref, self.g1_sem.at[t, d - 1, 0], self.g1_sem.at[t, d - 1, 1],
+                      self.place.along(o, (p + d) % 4))
+
+    def gather1_wait(self, t, o, d):
+        ref = self.rows(t, (self.place.xyz[o] + 4 - d) % 4)
+        return remote(ref, ref, self.g1_sem.at[t, d - 1, 0], self.g1_sem.at[t, d - 1, 1], self.place.other())
+
+    def gatherc_copy(self, t):
+        ref = self.out.at[t, pl.ds(self.place.core * HALF, HALF)]
+        return remote(ref, ref, self.gc_sem.at[t, 0], self.gc_sem.at[t, 1], self.place.other())
+
+    def gatherc_wait(self, t):
+        ref = self.out.at[t, pl.ds((1 - self.place.core) * HALF, HALF)]
+        return remote(ref, ref, self.gc_sem.at[t, 0], self.gc_sem.at[t, 1], self.place.other())
+
+    def step0(self, g):
+        for o in range(3):
+            t = 3 * g + o
+            self.c_out[t] = self.part[t, pl.ds((1 - self.place.core) * HALF, HALF)].astype(BF)
+            self.core_copy(t).start()
+
+    def step1(self, g):
+        for o in range(3):
+            t = 3 * g + o
+            self.core_copy(t).wait_recv()
+            mine = pl.ds(self.place.core * HALF, HALF)
+            total = self.part[t, mine] + self.c_in[t].astype(F32)
+            self.part[t, mine] = total
+            self.q_out[t] = total.astype(BF)
+            for d in (2, 1, 3):
+                self.quarter_copy(t, o, d).start()
+
+    def step2(self, g):
+        for o in range(3):
+            t = 3 * g + o
+            row = self.place.core * HALF + self.place.xyz[o] * QUART
+            total = self.part[t, pl.ds(row, QUART)]
+            for d in (1, 3, 2):
+                self.quarter_copy(t, o, d).wait_recv()
+                total = total + self.q_in[t, d - 1].astype(F32)
+            self.q_own[t] = total
+            self.s_out[t] = total.astype(BF)
+            p = self.place.xyz[(o + 1) % 3]
+
+            @pl.when(p != g)
+            def _():
+                self.second_copy(t, o, g, (p + 4 - g) % 4 - 1).start()
+
+    def step3(self, g):
+        for o in range(3):
+            t = 3 * g + o
+            p = self.place.xyz[(o + 1) % 3]
+
+            @pl.when(p == g)
+            def _():
+                total = self.q_own[t]
+                for slot in range(3):
+                    self.second_copy(t, o, g, slot).wait_recv()
+                    total = total + self.s_in[o, slot].astype(F32)
+                self.t_buf[o, self.place.xyz[(o + 2) % 3]] = total.astype(BF)
+                for d in (2, 1, 3):
+                    self.third_copy(o, d).start()
+
+    def step4(self, g):
+        for o in range(3):
+            t = 3 * g + o
+            p = self.place.xyz[(o + 1) % 3]
+
+            @pl.when(p == g)
+            def _():
+                for d in (1, 3, 2):
+                    self.third_wait(o, d).wait_recv()
+                buf = self.t_buf
+                total = (buf[o, 0].astype(F32) + buf[o, 1].astype(F32)) + (buf[o, 2].astype(F32) + buf[o, 3].astype(F32))
+                row = self.place.core * HALF + self.place.xyz[o] * QUART
+                self.out[t, pl.ds(row, QUART)] = total.astype(BF)
+                for d in (2, 1, 3):
+                    self.gather2_copy(t, o, d).start()
+
+    def step5(self, g):
+        for o in range(3):
+            t = 3 * g + o
+            p = self.place.xyz[(o + 1) % 3]
+
+            @pl.when(p != g)
+            def _():
+                self.gather2_copy(t, o, 1).wait_recv()
+
+            for d in (2, 1, 3):
+                self.gather1_copy(t, o, d).start()
+
+    def step6(self, g):
+        for o in range(3):
+            t = 3 * g + o
+            for d in (1, 3, 2):
+                self.gather1_wait(t, o, d).wait_recv()
+            self.gatherc_copy(t).start()
+
+    def step7(self, g):
+        for o in range(3):
+            self.gatherc_wait(3 * g + o).wait_recv()
+
+    def sends(self, g):
+        for o in range(3):
+            t = 3 * g + o
+            p = self.place.xyz[(o + 1) % 3]
+            self.core_copy(t).wait_send()
+            for d in (1, 2, 3):
+                self.quarter_copy(t, o, d).wait_send()
+                self.gather1_copy(t, o, d).wait_send()
+            self.gatherc_copy(t).wait_send()
+
+            @pl.when(p != g)
+            def _():
+                self.second_copy(t, o, g, (p + 4 - g) % 4 - 1).wait_send()
+
+            @pl.when(p == g)
+            def _():
+                for d in (1, 2, 3):
+                    self.third_copy(o, d).wait_send()
+                    self.gather2_copy(t, o, d).wait_send()
+
+
+def greet(place, halos):
+    barrier = pltpu.get_barrier_semaphore()
+    friends = [place.other()]
+    for axis in range(3):
+        for d in (1, 2, 3):
+            friends.append(place.along(axis, (place.xyz[axis] + d) % 4))
+    if halos:
+        friends.append(((place.tm + 1) % 4, place.height))
+        friends.append(((place.tm + 3) % 4, place.height))
+        friends.append((place.tm, (place.height + 1) % 32))
+        friends.append((place.tm, (place.height + 31) % 32))
+    for device in friends:
+        pl.semaphore_signal(barrier, inc=1, device_id=device, device_id_type=MESH)
+    pl.semaphore_wait(barrier, len(friends))
+
+
+def reduce_kernel(part_ref, out_ref, part, *refs):
+    place = Place()
+    greet(place, False)
+    part[...] = part_ref[...]
+    red = Reduce(place, part, out_ref, refs)
+    steps = [red.step0, red.step1, red.step2, red.step3, red.step4, red.step5, red.step6, red.step7, red.sends]
+    for step in steps:
+        @pl.loop(0, 4)
+        def _(g):
+            step(g)
+
+
+def reduced(partial):
+    return pl.pallas_call(
+        reduce_kernel,
+        out_shape=jax.ShapeDtypeStruct((12, 384, 384), BF),
+        in_specs=[pl.BlockSpec(memory_space=pltpu.VMEM)],
+        out_specs=pl.BlockSpec(memory_space=pltpu.VMEM),
+        scratch_shapes=[pltpu.VMEM((12, 384, 384), F32)] + Reduce.SCRATCH,
+        compiler_params=pltpu.CompilerParams(
+            collective_id=0, has_side_effects=True, vmem_limit_bytes=56 * 2**20),
+    )(partial)
 
 
 def shifted(array, axis, by):
@@ -76,10 +339,8 @@
     for tap in range(3):
         total = total + backward(flat(after[tap : tap + frames]), temporal_weight[tap])
     latent_grad = total.reshape(frames, rows, cols, chans).astype(jnp.bfloat16)
-    temporal_local = jnp.stack(temporal)
-    spatial_local = jnp.stack(spatial).reshape(3, 3, chans, chans)
-    temporal_sum, spatial_sum = lax.psum((temporal_local, spatial_local), ("tm", "height"))
-    return (latent_grad, temporal_sum * scale, spatial_sum * scale)
+    total = reduced(jnp.stack(spatial + temporal)).astype(jnp.float32) * scale
+    return (latent_grad, total[9:], total[:9].reshape(3, 3, chans, chans))
 
 
 def solution(mesh):

time: 285 us -> 163 us (0.57)
  waiting for transfers between devices: 172 us -> 17.5 us
  Pallas kernels: 0 us -> 47.7 us
  between operations: 14.4 us -> 0.87 us
  matrix products: 61.3 us -> 67.5 us
  other arithmetic: 13.2 us -> 7.35 us
    psum x1 -> x0, waiting for transfers between devices: 135 us -> none  [on_device(): lax.psum((temporal_local, spatial_local), ('tm', 'height'))]
    pallas_call x0 -> x1, Pallas kernels: none -> 47.7 us  [reduced(): pl.pallas_call(reduce_kernel, out_shape=jax.ShapeDtypeStruct((12, 384, 38...]
    ppermute x2, waiting for transfers between devices: 25.5 us -> 0.01 us  [shifted(): return lax.ppermute(array, axis, pairs)]
    ppermute x1, waiting for transfers between devices: 0.87 us -> 13.6 us  [extended(): before = lax.ppermute(last, axis, up)]
    dot_general x12, matrix products: 18.4 us -> 27.7 us  [inner(): lax.dot_general(left, right, (((0,), (0,)), ((), ())), preferred_element_...]
    ppermute x1, waiting for transfers between devices: 11.3 us -> 3.86 us  [extended(): after = lax.ppermute(first, axis, down)]
    mul x2 -> x1, other arithmetic: 6.97 us -> 2.73 us  [on_device(): total = reduced(jnp.stack(spatial + temporal)).astype(jnp.float32) * scale]
    unnamed x17 -> x14, local copies, waits for them, and re-layouts: 4.22 us -> 0.04 us
  transfers between devices with their start and end apart: 5 -> 4, of which waited for: 4 -> 2; matrix products, arithmetic and copies ran while one was open for 13% -> 39% of each run, Pallas kernels for 0% -> 29%
where the time goes in v1:
time: 163 us; the launch traced here: 162 us
  matrix products  67.5 us (41%)
  Pallas kernels  47.7 us (29%)
  waiting for transfers between devices  17.5 us (11%)
  starting transfers between devices  13.1 us (8%)
  local copies, waits for them, and re-layouts  8.42 us (5%)
  other arithmetic  7.35 us (5%)
    pallas_call x1, Pallas kernels, reduced(): pl.pallas_call(reduce_kernel, out_shape=jax.ShapeDtypeStruct((12, 384, 38...  47.7 us
    dot_general x12, matrix products, backward(): lax.dot_general(left, weight, (((1,), (1,)), ((), ())), preferred_element...  30.7 us
    dot_general x12, matrix products, inner(): lax.dot_general(left, right, (((0,), (0,)), ((), ())), preferred_element_...  27.7 us
    ppermute x1, waiting for transfers between devices, extended(): before = lax.ppermute(last, axis, up)  13.6 us
    dot_general x3, matrix products, on_device(): jnp.dot(flat(before[2 - tap:2 - tap + frames]), temporal_weight[tap], pre...  9.03 us
    ppermute x2, starting transfers between devices, shifted(): return lax.ppermute(array, axis, pairs)  7.82 us
    slice x2, local copies, waits for them, and re-layouts, on_device(): return (latent_grad, total[9:], total[:9].reshape(3, 3, chans, chans))  4.08 us
    ppermute x1, starting transfers between devices, extended(): before = lax.ppermute(last, axis, up)  4.01 us
  transfers between devices with their start and end apart: 4, of which 2 were waited for; matrix products, arithmetic and copies ran while one was open for 39% of the time, Pallas kernels for 29%

profile of v1, /device:TPU:1, one launch (start us, length us, event | category | flops | bytes accessed | tf_op | source)
XLA Modules:
  0.0 162.5 jit_solution(9929707599500952020)
XLA Ops:
  0.6 0.0 copy-start.3
  0.7 1.9 %fusion.59 = (bf16[2,1,640,384]{3,2,1,0:T(8,128)(2,1)S(1)}, bf16[2,1,640,384]{3,2,1,0:T(8,128)(2,1)S(1)}) fusion(bf16[2,2,640,384]{3,2,1,0:T(8,128)(2,1)} %param.5), kind=kLoop, calls=%fused_computation.91 | loop fusion | bytes 3932160 | tf_op jit(solution)/shard_map/slice | solution.py:283
  2.5 4.0 %collective-permute-start = (bf16[2,1,640,384]{3,2,1,0:T(8,128)(2,1)S(1)}, bf16[2,1,640,384]{3,2,1,0:T(8,128)(2,1)S(1)}, u32[]{:S(2)}, u32[]{:S(2)}) collective-permute-start(bf16[2,1,640,384]{3,2,1,0:T(8,128)(2,1)S(1)} %get-tuple-element.11), channel_id=1, source_target_pairs={{0,1},{1,2},{2,3},{3,4},{4,5},{5,6},{6,7},{7,8},{8,9},{9,10},{10,1... | collective-permute-start | bytes 2949128 | tf_op jit(solution)/shard_map/ppermute | solution.py:285
  6.5 1.3 collective-permute-start.1
  7.8 4.0 %collective-permute-start.2 = (bf16[2,2,640,384]{3,2,1,0:T(8,128)(2,1)S(1)}, bf16[2,2,640,384]{3,2,1,0:T(8,128)(2,1)}, u32[]{:S(2)}, u32[]{:S(2)}) collective-permute-start(bf16[2,2,640,384]{3,2,1,0:T(8,128)(2,1)S(1)} %copy-done.1), channel_id=1, source_target_pairs={{0,32},{32,64},{64,96},{1,33},{33,65},{65,97},{2,34},{34,66},{66,9... | collective-permute-start | bytes 5898248 | tf_op jit(solution)/shard_map/ppermute | solution.py:275
  11.9 0.0 copy-start
  11.9 1.4 fusion.30
  13.3 13.6 %collective-permute-done = bf16[2,1,640,384]{3,2,1,0:T(8,128)(2,1)S(1)} collective-permute-done((bf16[2,1,640,384]{3,2,1,0:T(8,128)(2,1)S(1)}, bf16[2,1,640,384]{3,2,1,0:T(8,128)(2,1)S(1)}, u32[]{:S(2)}, u32[]{:S(2)}) %collective-permute-start) | collective-permute-done | bytes 983072 | tf_op jit(solution)/shard_map/ppermute | solution.py:285
  26.9 3.9 %collective-permute-done.1 = bf16[2,1,640,384]{3,2,1,0:T(8,128)(2,1)S(1)} collective-permute-done((bf16[2,1,640,384]{3,2,1,0:T(8,128)(2,1)S(1)}, bf16[2,1,640,384]{3,2,1,0:T(8,128)(2,1)S(1)}, u32[]{:S(2)}, u32[]{:S(2)}) %collective-permute-start.1) | collective-permute-done | bytes 983072 | tf_op jit(solution)/shard_map/ppermute | solution.py:286
  30.7 1.3 fusion.11
  32.0 2.4 %fusion.58 = (bf16[2,2,640,384]{3,2,1,0:T(8,128)(2,1)S(1)}, bf16[2,2,640,384]{3,2,1,0:T(8,128)(2,1)S(1)}, bf16[2,2,640,384]{3,2,1,0:T(8,128)(2,1)S(1)}, bf16[2,2...) fusion(bf16[2,4,642,384]{3,2,1,0:T(8,128)(2,1)S(1)} %fusion.11), kind=kLoop, calls=%fused_computation.90 | loop fusion | bytes 23592960 | tf_op jit(solution)/shard_map/slice | solution.py:327
  34.4 2.3 %fusion.41 = f32[2560,384]{1,0:T(8,128)S(1)} fusion(bf16[2560,384]{1,0:T(8,128)(2,1)S(1)} %bitcast.164, bf16[3,3,384,384]{3,2,1,0:T(8,128)(2,1)} %param.7), kind=kOutput, calls=%fused_computation.73 | convolution fusion | flops 754974720 | bytes 6193152 | tf_op jit(solution)/shard_map/dot_general | solution.py:302
  36.8 1.7 %pad_maximum_fusion.2 = (bf16[2,2,640,384]{3,2,1,0:T(8,128)(2,1)}, bf16[2,2,640,384]{3,2,1,0:T(8,128)(2,1)S(1)}) fusion(bf16[2,2,640,384]{3,2,1,0:T(8,128)(2,1)S(1)} %copy-done, bf16[2,1,640,384]{3,2,1,0:T(8,128)(2,1)S(1)} %collective-permute-done, bf16[2,1,640,384]{3,2,1,0:T(8,128)(2,1)S(1)} %collective-permute-done.1), kind=kLoop, calls=%fused_computation.30 | loop fusion | flops 1966080 | bytes 7864320 | tf_op jit(solution)/shard_map/concatenate | solution.py:287
  38.5 2.5 %convolution_add_fusion.10 = f32[2560,384]{1,0:T(8,128)S(1)} fusion(f32[2560,384]{1,0:T(8,128)S(1)} %fusion.41, bf16[2560,384]{1,0:T(8,128)(2,1)S(1)} %bitcast.174, bf16[3,3,384,384]{3,2,1,0:T(8,128)(2,1)} %param.7), kind=kOutput, calls=%fused_computation.21 | convolution fusion | flops 755957760 | bytes 10125312 | tf_op jit(solution)/shard_map/dot_general | solution.py:302
  41.0 2.4 %convolution_add_fusion.9 = f32[2560,384]{1,0:T(8,128)S(1)} fusion(f32[2560,384]{1,0:T(8,128)S(1)} %convolution_add_fusion.10, bf16[2560,384]{1,0:T(8,128)(2,1)S(1)} %bitcast.172, bf16[3,3,384,384]{3,2,1,0:T(8,128)(2,1)} %param.7), kind=kOutput, calls=%fused_computation.20 | convolution fusion | flops 755957760 | bytes 10125312 | tf_op jit(solution)/shard_map/dot_general | solution.py:302
  43.4 2.3 %fusion.32 = f32[2560,384]{1,0:T(8,128)S(1)} fusion(bf16[2560,384]{1,0:T(8,128)(2,1)S(1)} %bitcast.161, bf16[3,3,384,384]{3,2,1,0:T(8,128)(2,1)} %param.7), kind=kOutput, calls=%fused_computation.64 | convolution fusion | flops 754974720 | bytes 6193152 | tf_op jit(solution)/shard_map/dot_general | solution.py:302
  45.7 2.4 %convolution_add_fusion.8 = f32[2560,384]{1,0:T(8,128)S(1)} fusion(f32[2560,384]{1,0:T(8,128)S(1)} %convolution_add_fusion.9, bf16[2560,384]{1,0:T(8,128)(2,1)S(1)} %bitcast.170, bf16[3,3,384,384]{3,2,1,0:T(8,128)(2,1)} %param.7), kind=kOutput, calls=%fused_computation.19 | convolution fusion | flops 755957760 | bytes 10125312 | tf_op jit(solution)/shard_map/dot_general | solution.py:302
  48.1 2.4 %convolution_add_fusion.7 = f32[2560,384]{1,0:T(8,128)S(1)} fusion(f32[2560,384]{1,0:T(8,128)S(1)} %convolution_add_fusion.8, bf16[2560,384]{1,0:T(8,128)(2,1)S(1)} %bitcast.152, bf16[3,3,384,384]{3,2,1,0:T(8,128)(2,1)} %param.7), kind=kOutput, calls=%fused_computation.18 | convolution fusion | flops 755957760 | bytes 10125312 | tf_op jit(solution)/shard_map/dot_general | solution.py:302
  50.5 2.4 %convolution_add_fusion.6 = f32[2560,384]{1,0:T(8,128)S(1)} fusion(f32[2560,384]{1,0:T(8,128)S(1)} %convolution_add_fusion.7, bf16[2560,384]{1,0:T(8,128)(2,1)S(1)} %bitcast.168, bf16[3,3,384,384]{3,2,1,0:T(8,128)(2,1)} %param.7), kind=kOutput, calls=%fused_computation.17 | convolution fusion | flops 755957760 | bytes 10125312 | tf_op jit(solution)/shard_map/dot_general | solution.py:302
  52.9 4.4 %convolution_add_fusion.5 = f32[2560,384]{1,0:T(8,128)} fusion(f32[2560,384]{1,0:T(8,128)S(1)} %convolution_add_fusion.6, bf16[2560,384]{1,0:T(8,128)(2,1)S(1)} %bitcast.166, bf16[3,3,384,384]{3,2,1,0:T(8,128)(2,1)} %param.7), kind=kOutput, calls=%fused_computation.16 | convolution fusion | flops 755957760 | bytes 10125312 | tf_op jit(solution)/shard_map/dot_general | solution.py:302
  57.3 1.4 pad_maximum_fusion.1
  58.7 1.4 convolution_add_fusion.3
  60.1 0.0 copy-start.2
  60.2 0.0 copy-start.5
  60.2 6.3 %multiply_convert_fusion = (bf16[2560,384]{1,0:T(8,128)(2,1)}, f32[2560,384]{1,0:T(8,128)}) fusion(f32[2560,384]{1,0:T(8,128)S(1)} %convolution_add_fusion.3, bf16[2560,384]{1,0:T(8,128)(2,1)} %bitcast.22, bf16[3,384,384]{2,1,0:T(8,128)(2,1)S(1)} %copy-done.3), kind=kOutput, calls=%fused_computation.26 | convolution fusion | flops 760872960 | bytes 12091392 | tf_op jit(solution)/shard_map/dot_general | solution.py:315
  66.4 4.3 %fusion.8 = bf16[2560,384]{1,0:T(8,128)(2,1)S(1)} fusion(f32[2560,384]{1,0:T(8,128)S(1)} %fusion.32, f32[2560,384]{1,0:T(8,128)S(1)} %copy-done.2, bf16[2560,384]{1,0:T(8,128)(2,1)S(1)} %bitcast.179, f32[2560,384]{1,0:T(8,128)} %get-tuple-element.14, bf16[3,3,384,384]{3,2,1,0:T(8,128)(2,1)} %param.7), kind=kOutput, calls=%fused_computation.22 | convolution fusion | flops 765788160 | bytes 16023552 | tf_op jit(solution)/shard_map/dot_general | solution.py:302
  70.7 3.8 %collective-permute-start.3 = (bf16[2,2,640,384]{3,2,1,0:T(8,128)(2,1)S(1)}, bf16[2,2,640,384]{3,2,1,0:T(8,128)(2,1)S(1)}, u32[]{:S(2)}, u32[]{:S(2)}) collective-permute-start(bf16[2,2,640,384]{3,2,1,0:T(8,128)(2,1)S(1)} %bitcast.157), channel_id=1, source_target_pairs={{32,0},{64,32},{96,64},{33,1},{65,33},{97,65},{34,2},{66,34},{98,6... | collective-permute-start | bytes 5898248 | tf_op jit(solution)/shard_map/ppermute | solution.py:275
  74.5 3.7 %fusion.23 = f32[12,384,384]{2,1,0:T(8,128)} fusion(bf16[2560,384]{1,0:T(8,128)(2,1)} %get-tuple-element.13, bf16[2560,384]{1,0:T(8,128)(2,1)S(1)} %bitcast.165), kind=kOutput, calls=%fused_computation.55 | convolution fusion | flops 754974720 | bytes 4521984 | tf_op jit(solution)/shard_map/dot_general | solution.py:296
  78.2 2.0 %fusion.22 = f32[12,384,384]{2,1,0:T(8,128)} fusion(f32[12,384,384]{2,1,0:T(8,128)} %fusion.23, bf16[2560,384]{1,0:T(8,128)(2,1)S(1)} %copy-done.6, bf16[2560,384]{1,0:T(8,128)(2,1)S(1)} %bitcast.175), kind=kOutput, calls=%fused_computation.53 | convolution fusion | flops 754974720 | bytes 4521984 | tf_op jit(solution)/shard_map/dot_general | solution.py:296
  80.3 2.1 %fusion.21 = f32[12,384,384]{2,1,0:T(8,128)} fusion(f32[12,384,384]{2,1,0:T(8,128)} %fusion.22, bf16[2560,384]{1,0:T(8,128)(2,1)S(1)} %copy-done.6, bf16[2560,384]{1,0:T(8,128)(2,1)S(1)} %bitcast.173), kind=kOutput, calls=%fused_computation.51 | convolution fusion | flops 754974720 | bytes 4521984 | tf_op jit(solution)/shard_map/dot_general | solution.py:296
  82.3 2.0 %fusion.20 = f32[12,384,384]{2,1,0:T(8,128)} fusion(f32[12,384,384]{2,1,0:T(8,128)} %fusion.21, bf16[2560,384]{1,0:T(8,128)(2,1)S(1)} %copy-done.6, bf16[2560,384]{1,0:T(8,128)(2,1)S(1)} %bitcast.171), kind=kOutput, calls=%fused_computation.49 | convolution fusion | flops 754974720 | bytes 4521984 | tf_op jit(solution)/shard_map/dot_general | solution.py:296
  84.4 2.0 %fusion.19 = f32[12,384,384]{2,1,0:T(8,128)} fusion(f32[12,384,384]{2,1,0:T(8,128)} %fusion.20, bf16[2560,384]{1,0:T(8,128)(2,1)S(1)} %copy-done.6, bf16[2560,384]{1,0:T(8,128)(2,1)S(1)} %bitcast.153), kind=kOutput, calls=%fused_computation.47 | convolution fusion | flops 754974720 | bytes 4521984 | tf_op jit(solution)/shard_map/dot_general | solution.py:296
  86.4 2.0 %fusion.18 = f32[12,384,384]{2,1,0:T(8,128)} fusion(f32[12,384,384]{2,1,0:T(8,128)} %fusion.19, bf16[2560,384]{1,0:T(8,128)(2,1)S(1)} %copy-done.6, bf16[2560,384]{1,0:T(8,128)(2,1)S(1)} %bitcast.169), kind=kOutput, calls=%fused_computation.45 | convolution fusion | flops 754974720 | bytes 4521984 | tf_op jit(solution)/shard_map/dot_general | solution.py:296
  88.4 2.0 %fusion.17 = f32[12,384,384]{2,1,0:T(8,128)} fusion(f32[12,384,384]{2,1,0:T(8,128)} %fusion.18, bf16[2560,384]{1,0:T(8,128)(2,1)S(1)} %copy-done.6, bf16[2560,384]{1,0:T(8,128)(2,1)S(1)} %bitcast.167), kind=kOutput, calls=%fused_computation.43 | convolution fusion | flops 754974720 | bytes 4521984 | tf_op jit(solution)/shard_map/dot_general | solution.py:296
  90.4 2.0 %fusion.16 = f32[12,384,384]{2,1,0:T(8,128)} fusion(f32[12,384,384]{2,1,0:T(8,128)} %fusion.17, bf16[2560,384]{1,0:T(8,128)(2,1)S(1)} %copy-done.6, bf16[2560,384]{1,0:T(8,128)(2,1)S(1)} %bitcast.180), kind=kOutput, calls=%fused_computation.41 | convolution fusion | flops 754974720 | bytes 4521984 | tf_op jit(solution)/shard_map/dot_general | solution.py:296
  92.5 2.0 %fusion.15 = f32[12,384,384]{2,1,0:T(8,128)} fusion(f32[12,384,384]{2,1,0:T(8,128)} %fusion.16, bf16[2560,384]{1,0:T(8,128)(2,1)S(1)} %copy-done.6, bf16[2560,384]{1,0:T(8,128)(2,1)S(1)} %bitcast.162), kind=kOutput, calls=%fused_computation.39 | convolution fusion | flops 754974720 | bytes 4521984 | tf_op jit(solution)/shard_map/dot_general | solution.py:296
  94.5 2.1 %fusion.14 = f32[12,384,384]{2,1,0:T(8,128)} fusion(f32[12,384,384]{2,1,0:T(8,128)} %fusion.15, bf16[2560,384]{1,0:T(8,128)(2,1)S(1)} %fusion.8, bf16[2560,384]{1,0:T(8,128)(2,1)S(1)} %bitcast.160), kind=kOutput, calls=%fused_computation.37 | convolution fusion | flops 754974720 | bytes 4521984 | tf_op jit(solution)/shard_map/dot_general | solution.py:296
  96.6 2.0 %fusion.13 = f32[12,384,384]{2,1,0:T(8,128)} fusion(f32[12,384,384]{2,1,0:T(8,128)} %fusion.14, bf16[2560,384]{1,0:T(8,128)(2,1)S(1)} %bitcast.156, bf16[2560,384]{1,0:T(8,128)(2,1)S(1)} %fusion.8), kind=kOutput, calls=%fused_computation.35 | convolution fusion | flops 754974720 | bytes 4521984 | tf_op jit(solution)/shard_map/dot_general | solution.py:296
  98.6 3.6 %fusion.12.part_ref = f32[12,384,384]{2,1,0:T(8,128)} fusion(f32[12,384,384]{2,1,0:T(8,128)} %fusion.13, bf16[2560,384]{1,0:T(8,128)(2,1)S(1)} %fusion.8, bf16[2560,384]{1,0:T(8,128)(2,1)} %bitcast.22), kind=kOutput, calls=%fused_computation.33 | convolution fusion | flops 754974720 | bytes 4521984 | tf_op jit(solution)/shard_map/dot_general | solution.py:296
  102.2 47.7 %shard_map.67 = bf16[12,384,384]{2,1,0:T(8,128)(2,1)} custom-call(f32[12,384,384]{2,1,0:T(8,128)} %fusion.12.part_ref), custom_call_target="tpu_custom_call" | custom-call | tf_op jit(solution)/shard_map/pallas_call | solution.py:261
  150.0 2.7 %convert_multiply_fusion = f32[12,384,384]{2,1,0:T(8,128)S(1)} fusion(bf16[12,384,384]{2,1,0:T(8,128)(2,1)} %shard_map.67), kind=kLoop, calls=%fused_computation.3 | loop fusion | flops 3538944 | bytes 10616832 | tf_op jit(solution)/shard_map/mul | solution.py:342
  152.7 1.3 slice.120
  154.1 2.8 %slice.121 = f32[9,384,384]{2,1,0:T(8,128)} slice(f32[12,384,384]{2,1,0:T(8,128)S(1)} %convert_multiply_fusion), slice={[0:9], [0:384], [0:384]} | slice | bytes 10616832 | tf_op jit(solution)/shard_map/slice | solution.py:343
  156.8 1.4 convolution_add_fusion.1
  158.2 0.0 collective-permute-done.3
  158.2 1.4 fusion.24
  159.6 0.2 pad_maximum_fusion
  159.8 2.7 %fusion.9 = bf16[2560,384]{1,0:T(8,128)(2,1)} fusion(f32[2560,384]{1,0:T(8,128)S(1)} %fusion.24, f32[2560,384]{1,0:T(8,128)S(1)} %convolution_add_fusion.1, bf16[2560,384]{1,0:T(8,128)(2,1)S(1)} %bitcast.176, bf16[3,384,384]{2,1,0:T(8,128)(2,1)S(1)} %copy-done.4), kind=kOutput, calls=%fused_computation.23 | convolution fusion | flops 757923840 | bytes 12091392 | tf_op jit(solution)/shard_map/dot_general | solution.py:302
  (11 shorter events, 0.0 us)
Async XLA Ops:
  0.6 7.2 %copy-start.1 = (bf16[2,2,640,384]{3,2,1,0:T(8,128)(2,1)S(1)}, bf16[2,2,640,384]{3,2,1,0:T(8,128)(2,1)}, u32[]{:S(2)}) copy-start(bf16[2,2,640,384]{3,2,1,0:T(8,128)(2,1)} %param.4) | copy-start | bytes 5898244
  0.6 11.3 %copy-start.3 = (bf16[3,384,384]{2,1,0:T(8,128)(2,1)S(1)}, bf16[3,384,384]{2,1,0:T(8,128)(2,1)}, u32[]{:S(2)}) copy-start(bf16[3,384,384]{2,1,0:T(8,128)(2,1)} %param.6) | copy-start | bytes 2654212
  2.5 24.4 %collective-permute-start = (bf16[2,1,640,384]{3,2,1,0:T(8,128)(2,1)S(1)}, bf16[2,1,640,384]{3,2,1,0:T(8,128)(2,1)S(1)}, u32[]{:S(2)}, u32[]{:S(2)}) collective-permute-start(bf16[2,1,640,384]{3,2,1,0:T(8,128)(2,1)S(1)} %get-tuple-element.11), channel_id=1, source_target_pairs={{0,1},{1,2},{2,3},{3,4},{4,5},{5,6},{6,7},{7,8},{8,9},{9,10},{10,1... | collective-permute-start | bytes 2949128 | tf_op jit(solution)/shard_map/ppermute | solution.py:285
  6.5 24.2 %collective-permute-start.1 = (bf16[2,1,640,384]{3,2,1,0:T(8,128)(2,1)S(1)}, bf16[2,1,640,384]{3,2,1,0:T(8,128)(2,1)S(1)}, u32[]{:S(2)}, u32[]{:S(2)}) collective-permute-start(bf16[2,1,640,384]{3,2,1,0:T(8,128)(2,1)S(1)} %get-tuple-element.12), channel_id=1, source_target_pairs={{1,0},{2,1},{3,2},{4,3},{5,4},{6,5},{7,6},{8,7},{9,8},{10,9},{11,1... | collective-permute-start | bytes 2949128 | tf_op jit(solution)/shard_map/ppermute | solution.py:286
  7.8 49.5 %collective-permute-start.2 = (bf16[2,2,640,384]{3,2,1,0:T(8,128)(2,1)S(1)}, bf16[2,2,640,384]{3,2,1,0:T(8,128)(2,1)}, u32[]{:S(2)}, u32[]{:S(2)}) collective-permute-start(bf16[2,2,640,384]{3,2,1,0:T(8,128)(2,1)S(1)} %copy-done.1), channel_id=1, source_target_pairs={{0,32},{32,64},{64,96},{1,33},{33,65},{65,97},{2,34},{34,66},{66,9... | collective-permute-start | bytes 5898248 | tf_op jit(solution)/shard_map/ppermute | solution.py:275
  11.9 18.8 %copy-start = (bf16[2,2,640,384]{3,2,1,0:T(8,128)(2,1)S(1)}, bf16[2,2,640,384]{3,2,1,0:T(8,128)(2,1)}, u32[]{:S(2)}) copy-start(bf16[2,2,640,384]{3,2,1,0:T(8,128)(2,1)} %param.5) | copy-start | bytes 5898244
  60.1 6.3 %copy-start.2 = (f32[2560,384]{1,0:T(8,128)S(1)}, f32[2560,384]{1,0:T(8,128)}, u32[]{:S(2)}) copy-start(f32[2560,384]{1,0:T(8,128)} %convolution_add_fusion.5) | copy-start | bytes 11796484
  60.2 6.3 %copy-start.5 = (bf16[2,2,640,384]{3,2,1,0:T(8,128)(2,1)S(1)}, bf16[2,2,640,384]{3,2,1,0:T(8,128)(2,1)}, u32[]{:S(2)}) copy-start(bf16[2,2,640,384]{3,2,1,0:T(8,128)(2,1)} %get-tuple-element.9) | copy-start | bytes 5898244
  70.7 87.5 %collective-permute-start.3 = (bf16[2,2,640,384]{3,2,1,0:T(8,128)(2,1)S(1)}, bf16[2,2,640,384]{3,2,1,0:T(8,128)(2,1)S(1)}, u32[]{:S(2)}, u32[]{:S(2)}) collective-permute-start(bf16[2,2,640,384]{3,2,1,0:T(8,128)(2,1)S(1)} %bitcast.157), channel_id=1, source_target_pairs={{32,0},{64,32},{96,64},{33,1},{65,33},{97,65},{34,2},{66,34},{98,6... | collective-permute-start | bytes 5898248 | tf_op jit(solution)/shard_map/ppermute | solution.py:275
  74.5 3.7 %copy-start.6 = (bf16[2560,384]{1,0:T(8,128)(2,1)S(1)}, bf16[2560,384]{1,0:T(8,128)(2,1)}, u32[]{:S(2)}) copy-start(bf16[2560,384]{1,0:T(8,128)(2,1)} %get-tuple-element.13) | copy-start | bytes 5898244
  154.1 2.8 %copy-start.4 = (bf16[3,384,384]{2,1,0:T(8,128)(2,1)S(1)}, bf16[3,384,384]{2,1,0:T(8,128)(2,1)}, u32[]{:S(2)}) copy-start(bf16[3,384,384]{2,1,0:T(8,128)(2,1)} %param.6) | copy-start | bytes 2654212

commit v2 on v1

--- a/solution.py
+++ b/solution.py
@@ -124,16 +124,16 @@
     def step0(self, g):
         for o in range(3):
             t = 3 * g + o
-            self.c_out[t] = self.part[t, pl.ds((1 - self.place.core) * HALF, HALF)].astype(BF)
+            self.c_out[t] = self.part[g, pl.ds((1 - self.place.core) * HALF, HALF), o * 384:(o + 1) * 384].astype(BF)
             self.core_copy(t).start()
 
     def step1(self, g):
         for o in range(3):
             t = 3 * g + o
             self.core_copy(t).wait_recv()
-            mine = pl.ds(self.place.core * HALF, HALF)
-            total = self.part[t, mine] + self.c_in[t].astype(F32)
-            self.part[t, mine] = total
+            mine = (g, pl.ds(self.place.core * HALF, HALF), slice(o * 384, (o + 1) * 384))
+            total = self.part[mine] + self.c_in[t].astype(F32)
+            self.part[mine] = total
             self.q_out[t] = total.astype(BF)
             for d in (2, 1, 3):
                 self.quarter_copy(t, o, d).start()
@@ -142,7 +142,7 @@
         for o in range(3):
             t = 3 * g + o
             row = self.place.core * HALF + self.place.xyz[o] * QUART
-            total = self.part[t, pl.ds(row, QUART)]
+            total = self.part[g, pl.ds(row, QUART), o * 384:(o + 1) * 384]
             for d in (1, 3, 2):
                 self.quarter_copy(t, o, d).wait_recv()
                 total = total + self.q_in[t, d - 1].astype(F32)
@@ -245,102 +245,295 @@
     pl.semaphore_wait(barrier, len(friends))
 
 
-def reduce_kernel(part_ref, out_ref, part, *refs):
+BOUNDS = (0, 144, 272, 400, 528, 640)
+CHUNKS = 5
+CW = 128
+
+
+def nt(left, right):
+    return lax.dot_general(left, right, (((1,), (1,)), ((), ())), preferred_element_type=F32)
+
+
+def tn(left, right):
+    return lax.dot_general(left, right, (((0,), (0,)), ((), ())), preferred_element_type=F32)
+
+
+def lanes(*values):
+    return jnp.concatenate(values, axis=1)
+
+
+def shifts(cot3, row, f, start, size):
+    low, high = max(start - 16, 0), min(start + size + 16, 640)
+    n = high - low
+    for b in range(3):
+        x = cot3[row, f, low:high, 384 + b * 128:384 + (b + 1) * 128].astype(F32)
+        place = lax.broadcasted_iota(jnp.int32, (n, 128), 0)
+        after = pltpu.roll(x, n - 1, 0)
+        before = pltpu.roll(x, 1, 0)
+        if high == 640:
+            after = jnp.where(place == n - 1, 0.0, after)
+        if low == 0:
+            before = jnp.where(place == 0, 0.0, before)
+        at = start - low
+        cot3[row, f, start:start + size, b * 128:(b + 1) * 128] = after[at:at + size].astype(BF)
+        cot3[row, f, start:start + size, 768 + b * 128:768 + (b + 1) * 128] = before[at:at + size].astype(BF)
+
+
+def block_kernel(lat_hbm, cot_hbm, tw_hbm, sw_hbm, lg_hbm, tg_hbm, sg_hbm,
+                 lat, cot3, back, hid, pgx, tw, twt, sw, part, out, lg,
+                 in_sem, w_sem, l_sem, u_sem, d_sem, p_sem, o_sem, *refs):
     place = Place()
-    greet(place, False)
-    part[...] = part_ref[...]
-    red = Reduce(place, part, out_ref, refs)
-    steps = [red.step0, red.step1, red.step2, red.step3, red.step4, red.step5, red.step6, red.step7, red.sends]
-    for step in steps:
-        @pl.loop(0, 4)
-        def _(g):
-            step(g)
-
-
-def reduced(partial):
-    return pl.pallas_call(
-        reduce_kernel,
-        out_shape=jax.ShapeDtypeStruct((12, 384, 384), BF),
-        in_specs=[pl.BlockSpec(memory_space=pltpu.VMEM)],
-        out_specs=pl.BlockSpec(memory_space=pltpu.VMEM),
-        scratch_shapes=[pltpu.VMEM((12, 384, 384), F32)] + Reduce.SCRATCH,
-        compiler_params=pltpu.CompilerParams(
-            collective_id=0, has_side_effects=True, vmem_limit_bytes=56 * 2**20),
-    )(partial)
-
-
-def shifted(array, axis, by):
-    size = lax.axis_size(axis)
-    pairs = [(i, i + by) for i in range(size) if 0 <= i + by < size]
-    return lax.ppermute(array, axis, pairs)
-
-
-def extended(array, sides, width):
-    for axis, dim in sides:
-        size, length = (lax.axis_size(axis), array.shape[dim])
-        up = [(i, (i + 1) % size) for i in range(size - 1)]
-        down = [(j, i) for i, j in up]
-        last = lax.slice_in_dim(array, length - width, length, axis=dim)
-        first = lax.slice_in_dim(array, 0, width, axis=dim)
-        before = lax.ppermute(last, axis, up)
-        after = lax.ppermute(first, axis, down)
-        array = jnp.concatenate([before, array, after], axis=dim)
-    return array
-
-
-def flat(value):
-    return value.reshape(-1, value.shape[-1])
-
-
-def inner(left, right):
-    return lax.dot_general(
-        left, right, (((0,), (0,)), ((), ())), preferred_element_type=jnp.float32
-    )
-
-
-def backward(left, weight):
-    return lax.dot_general(
-        left, weight, (((1,), (1,)), ((), ())), preferred_element_type=jnp.float32
-    )
+    tm, height = place.tm, place.height
+    cot_in = [pltpu.make_async_copy(cot_hbm.at[:, r], cot3.at[r + 1, :, :, 384:768], in_sem.at[r]) for r in range(2)]
+    lat_in = pltpu.make_async_copy(lat_hbm, lat.at[2:4], in_sem.at[2])
+    tw_in = pltpu.make_async_copy(tw_hbm, tw, in_sem.at[3])
+    sw_in = [pltpu.make_async_copy(sw_hbm.at[i, j], sw.at[i, :, j * 384:(j + 1) * 384], w_sem.at[3 * i + j])
+             for i in (1, 0, 2) for j in range(3)]
+    twt_in = [pltpu.make_async_copy(tw_hbm.at[k], twt.at[:, k * 384:(k + 1) * 384], w_sem.at[9 + k]) for k in range(3)]
+    for copy in cot_in + sw_in + [lat_in, tw_in] + twt_in:
+        copy.start()
+
+    greet(place, True)
+
+    def l_copy(c):
+        cols = pl.ds(c * CW, CW)
+        return remote(lat_hbm.at[:, :, cols], lat.at[0:2, :, cols], l_sem.at[c, 0], l_sem.at[c, 1],
+                      ((tm + 1) % 4, height))
+
+    def down_copy(c):
+        cols = pl.ds(BOUNDS[c], BOUNDS[c + 1] - BOUNDS[c])
+        return remote(cot_hbm.at[:, 1, cols], cot3.at[0, :, cols, 384:768], d_sem.at[c, 0], d_sem.at[c, 1],
+                      (tm, (height + 1) % 32))
+
+    def up_copy(c):
+        cols = pl.ds(BOUNDS[c], BOUNDS[c + 1] - BOUNDS[c])
+        return remote(cot_hbm.at[:, 0, cols], cot3.at[3, :, cols, 384:768], u_sem.at[c, 0], u_sem.at[c, 1],
+                      (tm, (height + 31) % 32))
+
+    def p_copy(c):
+        cols = pl.ds(c * CW, CW)
+        return remote(pgx.at[0:2, :, cols], pgx.at[2:4, :, cols], p_sem.at[c, 0], p_sem.at[c, 1],
+                      ((tm + 3) % 4, height))
+
+    for c in range(CHUNKS):
+        @pl.when(tm < 3)
+        def _():
+            l_copy(c).start()
+
+        @pl.when(height < 31)
+        def _():
+            down_copy(c).start()
+
+        @pl.when(height > 0)
+        def _():
+            up_copy(c).start()
+
+    @pl.when(tm == 0)
+    def _():
+        lat[0:2] = jnp.zeros((2, 2, 640, 384), BF)
+
+    @pl.when(tm == 3)
+    def _():
+        pgx[2:4] = jnp.zeros((2, 2, 640, 384), BF)
+
+    @pl.when(height == 0)
+    def _():
+        cot3[0, :, :, 384:768] = jnp.zeros((2, 640, 384), BF)
+
+    @pl.when(height == 31)
+    def _():
+        cot3[3, :, :, 384:768] = jnp.zeros((2, 640, 384), BF)
+
+    for copy in cot_in:
+        copy.wait()
+    for row in (1, 2):
+        for f in range(2):
+            shifts(cot3, row, f, 0, 640)
+    for copy in sw_in:
+        copy.wait()
+    for f in range(2):
+        back[0, f] = nt(lanes(cot3[1, f], cot3[2, f]), lanes(sw[1], sw[0]))
+        back[1, f] = nt(lanes(cot3[2, f], cot3[1, f]), lanes(sw[1], sw[2]))
+    lat_in.wait()
+    tw_in.wait()
+    for copy in twt_in:
+        copy.wait()
+
+    weight = tw.reshape(1152, 384)
+    for c in range(CHUNKS):
+        cols = slice(c * CW, (c + 1) * CW)
+
+        @pl.when(tm > 0)
+        def _():
+            l_copy(c).wait_recv()
+
+        @pl.when(height > 0)
+        def _():
+            down_copy(c).wait_recv()
+
+        @pl.when(height < 31)
+        def _():
+            up_copy(c).wait_recv()
+
+        for row in (0, 3):
+            for f in range(2):
+                shifts(cot3, row, f, c * CW, CW)
+        for r in range(2):
+            halo, i = (0, 2) if r == 0 else (3, 0)
+            window = jnp.concatenate([cot3[halo, f, cols] for f in range(2)], axis=0)
+            total = nt(window, sw[i]) + jnp.concatenate([back[r, f, cols] for f in range(2)], axis=0)
+            left = jnp.concatenate(
+                [lanes(lat[f + 2, r, cols], lat[f + 1, r, cols], lat[f, r, cols]) for f in range(2)], axis=0)
+            pre = jnp.dot(left, weight[...], preferred_element_type=F32)
+            sigma = jax.nn.sigmoid(pre)
+            hidden = (pre * sigma).astype(BF)
+            grad = (total * sigma * (1.0 + pre * (1.0 - sigma))).astype(BF)
+            for f in range(2):
+                hid[r, f, cols] = hidden[f * CW:(f + 1) * CW]
+                pgx[f, r, cols] = grad[f * CW:(f + 1) * CW]
+
+        @pl.when(tm > 0)
+        def _():
+            p_copy(c).start()
+
+    red = Reduce(place, part, out, refs)
+
+    def spatial(i, r):
+        value = tn(hid[r].reshape(1280, 384), cot3[r + 2 - i].reshape(1280, 1152))
+        part[i] = value if r == 0 else part[i] + value
+
+    def temporal(f):
+        grads = lanes(*(pgx[f + k].reshape(1280, 384) for k in range(3)))
+        value = tn(lat[f + 2].reshape(1280, 384), grads)
+        part[3] = value if f == 0 else part[3] + value
+
+    def latent(f, r):
+        grads = lanes(*(pgx[f + k, r] for k in range(3)))
+        lg[f, r] = (cot3[r + 1, f, :, 384:768].astype(F32) + nt(grads, twt[...])).astype(BF)
+        pltpu.make_async_copy(lg.at[f, r], lg_hbm.at[f, r], o_sem.at[4 + 2 * f + r]).start()
+
+    def store(g):
+        target = sg_hbm.at[g] if g < 3 else tg_hbm
+        return pltpu.make_async_copy(out.at[3 * g:3 * g + 3], target, o_sem.at[g])
+
+    def arrive():
+        for c in range(CHUNKS):
+            @pl.when(tm < 3)
+            def _():
+                p_copy(c).wait_recv()
+
+    def last(g):
+        red.step7(g)
+        store(g).start()
+
+    spatial(0, 0)
+    spatial(0, 1)
+    red.step0(0)
+    spatial(1, 0)
+    red.step1(0)
+    spatial(1, 1)
+    red.step0(1)
+    red.step2(0)
+    spatial(2, 0)
+    red.step1(1)
+    red.step3(0)
+    spatial(2, 1)
+    red.step0(2)
+    red.step2(1)
+    red.step4(0)
+    arrive()
+    temporal(0)
+    red.step1(2)
+    red.step3(1)
+    red.step5(0)
+    temporal(1)
+    red.step0(3)
+    red.step2(2)
+    red.step4(1)
+    red.step6(0)
+    latent(0, 0)
+    red.step1(3)
+    red.step3(2)
+    red.step5(1)
+    last(0)
+    latent(0, 1)
+    red.step2(3)
+    red.step4(2)
+    red.step6(1)
+    latent(1, 0)
+    red.step3(3)
+    red.step5(2)
+    last(1)
+    latent(1, 1)
+    red.step4(3)
+    red.step6(2)
+    red.step5(3)
+    last(2)
+    red.step6(3)
+    last(3)
+
+    for c in range(CHUNKS):
+        @pl.when(tm < 3)
+        def _():
+            l_copy(c).wait_send()
+
+        @pl.when(height < 31)
+        def _():
+            down_copy(c).wait_send()
+
+        @pl.when(height > 0)
+        def _():
+            up_copy(c).wait_send()
+
+        @pl.when(tm > 0)
+        def _():
+            p_copy(c).wait_send()
+    for g in range(4):
+        red.sends(g)
+        store(g).wait()
+    for f in range(2):
+        for r in range(2):
+            pltpu.make_async_copy(lg.at[f, r], lg_hbm.at[f, r], o_sem.at[4 + 2 * f + r]).wait()
 
 
 def on_device(latents, cotangent, temporal_weight, spatial_weight):
     frames, rows, cols, chans = latents.shape
     count = frames * lax.axis_size("tm") * rows * lax.axis_size("height") * cols
     scale = 1.0 / math.sqrt(count)
-    earlier = shifted(latents, "tm", 1)
-    before = jnp.concatenate([earlier, latents], axis=0)
-    pre = jnp.zeros((frames * rows * cols, chans), jnp.float32)
-    for tap in range(3):
-        pre = pre + jnp.dot(
-            flat(before[2 - tap : 2 - tap + frames]),
-            temporal_weight[tap],
-            preferred_element_type=jnp.float32,
-        )
-    hidden = jax.nn.silu(pre).astype(jnp.bfloat16)
-    rimmed = extended(cotangent, (("height", 1),), 1)
-    padded = jnp.pad(rimmed, ((0, 0), (0, 0), (1, 1), (0, 0)))
-    back = jnp.zeros((frames * rows * cols, chans), jnp.float32)
-    spatial = []
-    for i in range(3):
-        for j in range(3):
-            window = flat(padded[:, 2 - i : 2 - i + rows, 2 - j : 2 - j + cols])
-            back = back + backward(window, spatial_weight[i, j])
-            spatial.append(inner(hidden, window))
-    sigma = jax.nn.sigmoid(pre)
-    pre_grad = (back * sigma * (1.0 + pre * (1.0 - sigma))).astype(jnp.bfloat16)
-    grid = pre_grad.reshape(frames, rows, cols, chans)
-    temporal = []
-    for tap in range(3):
-        temporal.append(inner(flat(before[2 - tap : 2 - tap + frames]), pre_grad))
-    total = flat(cotangent).astype(jnp.float32)
-    later = shifted(grid, "tm", -1)
-    after = jnp.concatenate([grid, later], axis=0)
-    for tap in range(3):
-        total = total + backward(flat(after[tap : tap + frames]), temporal_weight[tap])
-    latent_grad = total.reshape(frames, rows, cols, chans).astype(jnp.bfloat16)
-    total = reduced(jnp.stack(spatial + temporal)).astype(jnp.float32) * scale
-    return (latent_grad, total[9:], total[:9].reshape(3, 3, chans, chans))
+    anywhere = pl.BlockSpec(memory_space=pl.ANY)
+    latent_grad, temporal, spatial = pl.pallas_call(
+        block_kernel,
+        out_shape=(
+            jax.ShapeDtypeStruct((2, 2, 640, 384), BF),
+            jax.ShapeDtypeStruct((3, 384, 384), BF),
+            jax.ShapeDtypeStruct((3, 3, 384, 384), BF),
+        ),
+        in_specs=[anywhere] * 4,
+        out_specs=(anywhere,) * 3,
+        scratch_shapes=[
+            pltpu.VMEM((4, 2, 640, 384), BF),
+            pltpu.VMEM((4, 2, 640, 1152), BF),
+            pltpu.VMEM((2, 2, 640, 384), F32),
+            pltpu.VMEM((2, 2, 640, 384), BF),
+            pltpu.VMEM((4, 2, 640, 384), BF),
+            pltpu.VMEM((3, 384, 384), BF),
+            pltpu.VMEM((384, 1152), BF),
+            pltpu.VMEM((3, 384, 1152), BF),
+            pltpu.VMEM((4, 384, 1152), F32),
+            pltpu.VMEM((12, 384, 384), BF),
+            pltpu.VMEM((2, 2, 640, 384), BF),
+            pltpu.SemaphoreType.DMA((4,)),
+            pltpu.SemaphoreType.DMA((12,)),
+            pltpu.SemaphoreType.DMA((CHUNKS, 2)),
+            pltpu.SemaphoreType.DMA((CHUNKS, 2)),
+            pltpu.SemaphoreType.DMA((CHUNKS, 2)),
+            pltpu.SemaphoreType.DMA((CHUNKS, 2)),
+            pltpu.SemaphoreType.DMA((8,)),
+        ] + Reduce.SCRATCH,
+        compiler_params=pltpu.CompilerParams(
+            collective_id=0, has_side_effects=True, vmem_limit_bytes=60 * 2**20),
+    )(latents, cotangent, temporal_weight, spatial_weight)
+    return (latent_grad, temporal.astype(F32) * scale, spatial.astype(F32) * scale)
 
 
 def solution(mesh):

time: 163 us -> 115 us (0.71)
  matrix products: 67.5 us -> 0 us
  Pallas kernels: 47.7 us -> 106 us
  waiting for transfers between devices: 17.5 us -> 0 us
  starting transfers between devices: 13.1 us -> 0 us
  local copies, waits for them, and re-layouts: 8.42 us -> 2.09 us
    dot_general x27 -> x0, matrix products: 67.5 us -> none  [the longest x12 30.7 us: backward(): lax.dot_general(left, weight, (((1,), (1,)), ((), ())), preferred_element...]
    pallas_call x1, Pallas kernels: 47.7 us -> 106 us  [on_device(): pl.pallas_call(block_kernel, out_shape=(jax.ShapeDtypeStruct((2, 2, 640,...]
    ppermute x4 -> x0, waiting for transfers between devices: 17.5 us -> none  [the longest x1 13.6 us: extended(): before = lax.ppermute(last, axis, up)]
    ppermute x4 -> x0, starting transfers between devices: 13.1 us -> none  [the longest x2 7.82 us: shifted(): return lax.ppermute(array, axis, pairs)]
    slice x4 -> x0, local copies, waits for them, and re-layouts: 8.38 us -> none  [the longest x2 4.08 us: on_device(): return (latent_grad, total[9:], total[:9].reshape(3, 3, chans, chans))]
    concatenate x4 -> x0, other arithmetic: 4.62 us -> none  [the longest x2 2.97 us: extended(): array = jnp.concatenate([before, array, after], axis=dim)]
    mul x1 -> x2, other arithmetic: 2.73 us -> 6.07 us  [the longest x1 4.7 us: on_device(): spatial.astype(F32) * scale]
    unnamed x14 -> x5, local copies, waits for them, and re-layouts: 0.04 us -> 2.09 us
  transfers between devices with their start and end apart: 4 -> 0, of which waited for: 2 -> 0; matrix products, arithmetic and copies ran while one was open for 39% -> 0% of each run, Pallas kernels for 29% -> 0%
where the time goes in v2:
time: 115 us
  Pallas kernels  106 us (92%)
  other arithmetic  6.07 us (5%)
  local copies, waits for them, and re-layouts  2.09 us (2%)
    pallas_call x1, Pallas kernels, on_device(): pl.pallas_call(block_kernel, out_shape=(jax.ShapeDtypeStruct((2, 2, 640,...  106 us
    mul x1, other arithmetic, on_device(): spatial.astype(F32) * scale  4.7 us

profile of v2, /device:TPU:1, one launch (start us, length us, event | category | flops | bytes accessed | tf_op | source)
XLA Modules:
  0.0 115.1 jit_solution(15669482501700367273)
XLA Ops:
  0.6 106.2 %shard_map.67 = (bf16[2,2,640,384]{3,2,1,0:T(8,128)(2,1)}, bf16[3,384,384]{2,1,0:T(8,128)(2,1)}, bf16[3,3,384,384]{3,2,1,0:T(8,128)(2,1)}) custom-call(bf16[2,2,640,384]{3,2,1,0:T(8,128)(2,1)} %lat_hbm.1, bf16[2,2,640,384]{3,2,1,0:T(8,128)(2,1)} %cot_hbm.1, bf16[3,384,384]{2,1,0:T(8,128)(2,1)} %tw_hbm.1, bf16[3,3,384,384]{3,2,1,0:T(8,128)(2,1)} %sw_hbm.1), custom_call_target="tpu_custom_call" | custom-call | tf_op jit(solution)/shard_map/pallas_call | solution.py:504
  106.9 0.0 copy-start.1
  106.9 4.7 %convert_multiply_fusion = f32[3,3,384,384]{3,2,1,0:T(8,128)} fusion(bf16[3,3,384,384]{3,2,1,0:T(8,128)(2,1)} %get-tuple-element.8), kind=kLoop, calls=%fused_computation | loop fusion | flops 2654208 | bytes 7962624 | tf_op jit(solution)/shard_map/mul | solution.py:536
  111.6 0.0 copy-start
  111.6 0.0 copy-done.1
  111.6 1.4 %convert_multiply_fusion.1 = f32[3,384,384]{2,1,0:T(8,128)} fusion(bf16[3,384,384]{2,1,0:T(8,128)(2,1)S(1)} %copy-done.1), kind=kLoop, calls=%fused_computation.1 | loop fusion | flops 884736 | bytes 2654208 | tf_op jit(solution)/shard_map/mul | solution.py:536
  113.0 0.8 copy-done
  113.8 1.3 %copy.8 = bf16[2,2,640,384]{3,2,1,0:T(8,128)(2,1)} copy(bf16[2,2,640,384]{3,2,1,0:T(8,128)(2,1)S(1)} %copy-done) | data formatting | bytes 3932160
Async XLA Ops:
  106.9 4.7 %copy-start.1 = (bf16[3,384,384]{2,1,0:T(8,128)(2,1)S(1)}, bf16[3,384,384]{2,1,0:T(8,128)(2,1)}, u32[]{:S(2)}) copy-start(bf16[3,384,384]{2,1,0:T(8,128)(2,1)} %get-tuple-element.7) | copy-start | bytes 2654212
  111.6 2.2 %copy-start = (bf16[2,2,640,384]{3,2,1,0:T(8,128)(2,1)S(1)}, bf16[2,2,640,384]{3,2,1,0:T(8,128)(2,1)}, u32[]{:S(2)}) copy-start(bf16[2,2,640,384]{3,2,1,0:T(8,128)(2,1)} %get-tuple-element.12) | copy-start | bytes 5898244

commit v3 on v2

--- a/solution.py
+++ b/solution.py
@@ -1,3 +1,4 @@
+import functools
 import math
 
 import jax
@@ -22,6 +23,12 @@
         self.height = height
         self.core = tm % 2
         self.xyz = (height % 4, (height // 16) * 2 + tm // 2, (height // 4) % 4)
+        x, y, z = self.xyz
+        self.corner = ((x == 0) | (x == 3)) & ((z == 0) | (z == 3))
+        self.diagonal = self.corner & (x == z)
+        self.half = height // 16
+        self.mirror = self.at(x, (y + 2) % 4, z, self.core)
+        self.opposite = self.at(3 - x, y, 3 - z, self.core)
 
     def at(self, x, y, z, core):
         return ((y % 2) * 2 + core, (y // 2) * 16 + z * 4 + x)
@@ -184,6 +191,8 @@
                 self.out[t, pl.ds(row, QUART)] = total.astype(BF)
                 for d in (2, 1, 3):
                     self.gather2_copy(t, o, d).start()
+                for d in (2, 1, 3):
+                    self.gather1_copy(t, o, d).start()
 
     def step5(self, g):
         for o in range(3):
@@ -193,9 +202,8 @@
             @pl.when(p != g)
             def _():
                 self.gather2_copy(t, o, 1).wait_recv()
-
-            for d in (2, 1, 3):
-                self.gather1_copy(t, o, d).start()
+                for d in (2, 1, 3):
+                    self.gather1_copy(t, o, d).start()
 
     def step6(self, g):
         for o in range(3):
@@ -242,12 +250,22 @@
         friends.append((place.tm, (place.height + 31) % 32))
     for device in friends:
         pl.semaphore_signal(barrier, inc=1, device_id=device, device_id_type=MESH)
-    pl.semaphore_wait(barrier, len(friends))
-
-
-BOUNDS = (0, 144, 272, 400, 528, 640)
-CHUNKS = 5
-CW = 128
+    if halos:
+        @pl.when(place.diagonal)
+        def _():
+            pl.semaphore_signal(barrier, inc=1, device_id=place.opposite, device_id_type=MESH)
+            pl.semaphore_wait(barrier, len(friends) + 1)
+
+        @pl.when(jnp.logical_not(place.diagonal))
+        def _():
+            pl.semaphore_wait(barrier, len(friends))
+    else:
+        pl.semaphore_wait(barrier, len(friends))
+
+
+BOUNDS = (0, 176, 336, 496, 640)
+CHUNKS = 4
+CW = 160
 
 
 def nt(left, right):
@@ -281,7 +299,7 @@
 
 def block_kernel(lat_hbm, cot_hbm, tw_hbm, sw_hbm, lg_hbm, tg_hbm, sg_hbm,
                  lat, cot3, back, hid, pgx, tw, twt, sw, part, out, lg,
-                 in_sem, w_sem, l_sem, u_sem, d_sem, p_sem, o_sem, *refs):
+                 in_sem, w_sem, l_sem, u_sem, d_sem, p_sem, o_sem, relay, r_sem, *refs):
     place = Place()
     tm, height = place.tm, place.height
     cot_in = [pltpu.make_async_copy(cot_hbm.at[:, r], cot3.at[r + 1, :, :, 384:768], in_sem.at[r]) for r in range(2)]
@@ -300,15 +318,70 @@
         return remote(lat_hbm.at[:, :, cols], lat.at[0:2, :, cols], l_sem.at[c, 0], l_sem.at[c, 1],
                       ((tm + 1) % 4, height))
 
-    def down_copy(c):
-        cols = pl.ds(BOUNDS[c], BOUNDS[c + 1] - BOUNDS[c])
-        return remote(cot_hbm.at[:, 1, cols], cot3.at[0, :, cols, 384:768], d_sem.at[c, 0], d_sem.at[c, 1],
+    def columns(c):
+        return pl.ds(BOUNDS[c], BOUNDS[c + 1] - BOUNDS[c])
+
+    def down_copy(c, f):
+        cols = columns(c)
+        return remote(cot_hbm.at[f, 1, cols], cot3.at[0, f, cols, 384:768], d_sem.at[c, f, 0], d_sem.at[c, f, 1],
                       (tm, (height + 1) % 32))
 
-    def up_copy(c):
-        cols = pl.ds(BOUNDS[c], BOUNDS[c + 1] - BOUNDS[c])
-        return remote(cot_hbm.at[:, 0, cols], cot3.at[3, :, cols, 384:768], u_sem.at[c, 0], u_sem.at[c, 1],
+    def up_copy(c, f):
+        cols = columns(c)
+        return remote(cot_hbm.at[f, 0, cols], cot3.at[3, f, cols, 384:768], u_sem.at[c, f, 0], u_sem.at[c, f, 1],
                       (tm, (height + 31) % 32))
+
+    x, y, z = place.xyz
+
+    def slot(way, c, f):
+        return relay.at[way, f, 0:BOUNDS[c + 1] - BOUNDS[c]]
+
+    def to_relay(way, c, f):
+        sem = (d_sem, u_sem)[way]
+        device = (place.mirror, place.opposite, place.at(3 - x, y, z, place.core), place.at(x, y, 3 - z, place.core))[c]
+        return remote(cot_hbm.at[f, 1 - way, columns(c)], slot(way, c, f), sem.at[c, f, 0], r_sem.at[way, f, 1], device)
+
+    def to_mirror(way, c, f):
+        return remote(slot(way, c, f), slot(way, c, f), r_sem.at[way, f, 0], r_sem.at[way, f, 1], place.mirror)
+
+    def to_band(way, c, f):
+        sem, row = ((d_sem, 0), (u_sem, 3))[way]
+        device = (place.opposite, place.mirror, place.at(x, y, 3 - z, place.core), place.at(3 - x, y, z, place.core))[c]
+        return remote(slot(way, c, f), cot3.at[row, f, columns(c), 384:768], r_sem.at[way, f, 0], sem.at[c, f, 1], device)
+
+    def here(way, c):
+        own = 3 - 3 * way
+        column = ((x == own) & (z == own), (x == 3 - own) & (z == 3 - own), (x == 3 - own) & (z == own),
+                  (x == own) & (z == 3 - own))[c]
+        return place.corner & column
+
+    def forward_first(f):
+        for way in range(2):
+            for c in range(1, 4):
+                @pl.when(here(way, c) & (place.half == way))
+                def _():
+                    to_mirror(way, c, f).wait_recv()
+                    (to_band if c == 1 else to_mirror)(way, c, f).start()
+
+    def forward_second(f):
+        for way in range(2):
+            for c in (0, 2, 3):
+                @pl.when(here(way, c) & (place.half == 1 - way))
+                def _():
+                    to_mirror(way, c, f).wait_recv()
+                    to_band(way, c, f).start()
+
+    def forward_sends(f):
+        for way in range(2):
+            for c in range(4):
+                @pl.when(here(way, c) & (place.half == (1 - way if c == 0 else way)))
+                def _():
+                    to_mirror(way, c, f).wait_send()
+
+            for c in (2, 3):
+                @pl.when(here(way, c) & (place.half == 1 - way))
+                def _():
+                    to_mirror(way, c, f).wait_send()
 
     def p_copy(c):
         cols = pl.ds(c * CW, CW)
@@ -316,17 +389,26 @@
                       ((tm + 3) % 4, height))
 
     for c in range(CHUNKS):
+        for f in range(2):
+            @pl.when(height == 15)
+            def _():
+                to_relay(0, c, f).start()
+
+            @pl.when(height == 16)
+            def _():
+                to_relay(1, c, f).start()
+
+            @pl.when((height < 31) & (height != 15))
+            def _():
+                down_copy(c, f).start()
+
+            @pl.when((height > 0) & (height != 16))
+            def _():
+                up_copy(c, f).start()
+
         @pl.when(tm < 3)
         def _():
             l_copy(c).start()
-
-        @pl.when(height < 31)
-        def _():
-            down_copy(c).start()
-
-        @pl.when(height > 0)
-        def _():
-            up_copy(c).start()
 
     @pl.when(tm == 0)
     def _():
@@ -353,27 +435,57 @@
         copy.wait()
     for f in range(2):
         back[0, f] = nt(lanes(cot3[1, f], cot3[2, f]), lanes(sw[1], sw[0]))
+        forward_first(f)
         back[1, f] = nt(lanes(cot3[2, f], cot3[1, f]), lanes(sw[1], sw[2]))
+    forward_second(0)
     lat_in.wait()
     tw_in.wait()
     for copy in twt_in:
         copy.wait()
 
+    def add(g, lanes_of, half, value):
+        part[g, :, lanes_of] = value if half == 0 else part[g, :, lanes_of] + value
+
+    def spatial(i, half):
+        cols = slice(half * 320, (half + 1) * 320)
+        value = tn(hid[:, :, cols].reshape(1280, 384), cot3[2 - i:4 - i, :, cols].reshape(1280, 1152))
+        add(i, slice(0, 1152), half, value)
+
+    def temporal(half):
+        cols = slice(half * 320, (half + 1) * 320)
+        grads = pgx[0:2, :, cols].reshape(1280, 384)
+        for k in range(3):
+            value = tn(lat[2 - k:4 - k, :, cols].reshape(1280, 384), grads)
+            add(3, slice(k * 384, (k + 1) * 384), half, value)
+
     weight = tw.reshape(1152, 384)
     for c in range(CHUNKS):
         cols = slice(c * CW, (c + 1) * CW)
+        if c == 1:
+            forward_second(1)
 
         @pl.when(tm > 0)
         def _():
             l_copy(c).wait_recv()
 
-        @pl.when(height > 0)
-        def _():
-            down_copy(c).wait_recv()
-
-        @pl.when(height < 31)
-        def _():
-            up_copy(c).wait_recv()
+        factors = []
+        for r in range(2):
+            left = jnp.concatenate(
+                [lanes(lat[f + 2, r, cols], lat[f + 1, r, cols], lat[f, r, cols]) for f in range(2)], axis=0)
+            pre = jnp.dot(left, weight[...], preferred_element_type=F32)
+            sigma = jax.nn.sigmoid(pre)
+            hidden = (pre * sigma).astype(BF)
+            for f in range(2):
+                hid[r, f, cols] = hidden[f * CW:(f + 1) * CW]
+            factors.append(sigma * (1.0 + pre * (1.0 - sigma)))
+        for f in range(2):
+            @pl.when(height > 0)
+            def _():
+                down_copy(c, f).wait_recv()
+
+            @pl.when(height < 31)
+            def _():
+                up_copy(c, f).wait_recv()
 
         for row in (0, 3):
             for f in range(2):
@@ -382,30 +494,20 @@
             halo, i = (0, 2) if r == 0 else (3, 0)
             window = jnp.concatenate([cot3[halo, f, cols] for f in range(2)], axis=0)
             total = nt(window, sw[i]) + jnp.concatenate([back[r, f, cols] for f in range(2)], axis=0)
-            left = jnp.concatenate(
-                [lanes(lat[f + 2, r, cols], lat[f + 1, r, cols], lat[f, r, cols]) for f in range(2)], axis=0)
-            pre = jnp.dot(left, weight[...], preferred_element_type=F32)
-            sigma = jax.nn.sigmoid(pre)
-            hidden = (pre * sigma).astype(BF)
-            grad = (total * sigma * (1.0 + pre * (1.0 - sigma))).astype(BF)
+            grad = (total * factors[r]).astype(BF)
             for f in range(2):
-                hid[r, f, cols] = hidden[f * CW:(f + 1) * CW]
                 pgx[f, r, cols] = grad[f * CW:(f + 1) * CW]
 
         @pl.when(tm > 0)
         def _():
             p_copy(c).start()
 
+        if c == 1:
+            for i in range(3):
+                spatial(i, 0)
+            temporal(0)
+
     red = Reduce(place, part, out, refs)
-
-    def spatial(i, r):
-        value = tn(hid[r].reshape(1280, 384), cot3[r + 2 - i].reshape(1280, 1152))
-        part[i] = value if r == 0 else part[i] + value
-
-    def temporal(f):
-        grads = lanes(*(pgx[f + k].reshape(1280, 384) for k in range(3)))
-        value = tn(lat[f + 2].reshape(1280, 384), grads)
-        part[3] = value if f == 0 else part[3] + value
 
     def latent(f, r):
         grads = lanes(*(pgx[f + k, r] for k in range(3)))
@@ -426,50 +528,46 @@
         red.step7(g)
         store(g).start()
 
-    spatial(0, 0)
     spatial(0, 1)
     red.step0(0)
-    spatial(1, 0)
+    spatial(1, 1)
     red.step1(0)
-    spatial(1, 1)
     red.step0(1)
+    spatial(2, 1)
+    red.step1(1)
+    red.step0(2)
+    temporal(1)
+    red.step1(2)
+    red.step0(3)
     red.step2(0)
-    spatial(2, 0)
-    red.step1(1)
+    red.step2(1)
+    red.step1(3)
+    red.step2(2)
+    arrive()
+    latent(0, 0)
+    red.step2(3)
+    latent(0, 1)
     red.step3(0)
-    spatial(2, 1)
-    red.step0(2)
-    red.step2(1)
+    red.step3(1)
+    red.step3(2)
+    red.step3(3)
+    latent(1, 0)
     red.step4(0)
-    arrive()
-    temporal(0)
-    red.step1(2)
-    red.step3(1)
+    red.step4(1)
+    red.step4(2)
+    red.step4(3)
+    latent(1, 1)
     red.step5(0)
-    temporal(1)
-    red.step0(3)
-    red.step2(2)
-    red.step4(1)
+    red.step5(1)
+    red.step5(2)
+    red.step5(3)
     red.step6(0)
-    latent(0, 0)
-    red.step1(3)
-    red.step3(2)
-    red.step5(1)
+    red.step6(1)
+    red.step6(2)
+    red.step6(3)
     last(0)
-    latent(0, 1)
-    red.step2(3)
-    red.step4(2)
-    red.step6(1)
-    latent(1, 0)
-    red.step3(3)
-    red.step5(2)
     last(1)
-    latent(1, 1)
-    red.step4(3)
-    red.step6(2)
-    red.step5(3)
     last(2)
-    red.step6(3)
     last(3)
 
     for c in range(CHUNKS):
@@ -477,23 +575,51 @@
         def _():
             l_copy(c).wait_send()
 
-        @pl.when(height < 31)
-        def _():
-            down_copy(c).wait_send()
-
-        @pl.when(height > 0)
-        def _():
-            up_copy(c).wait_send()
+        for f in range(2):
+            @pl.when(height < 31)
+            def _():
+                down_copy(c, f).wait_send()
+
+            @pl.when(height > 0)
+            def _():
+                up_copy(c, f).wait_send()
 
         @pl.when(tm > 0)
         def _():
             p_copy(c).wait_send()
+    for f in range(2):
+        forward_sends(f)
     for g in range(4):
         red.sends(g)
         store(g).wait()
     for f in range(2):
         for r in range(2):
             pltpu.make_async_copy(lg.at[f, r], lg_hbm.at[f, r], o_sem.at[4 + 2 * f + r]).wait()
+
+
+def scale_kernel(scale, lg_ref, tg_ref, sg_ref, lg_out, tg_out, sg_out):
+    lg_out[...] = lg_ref[...]
+    tg_out[...] = tg_ref[...].astype(F32) * scale
+    sg_out[...] = sg_ref[...].astype(F32) * scale
+
+
+def scaled(latent_grad, temporal, spatial, scale):
+    def blocks(rows):
+        return pl.BlockSpec((rows // 4, 384), lambda i: (i, 0))
+
+    latent_grad, temporal, spatial = pl.pallas_call(
+        functools.partial(scale_kernel, scale),
+        grid=(4,),
+        out_shape=(
+            jax.ShapeDtypeStruct((2560, 384), BF),
+            jax.ShapeDtypeStruct((1152, 384), F32),
+            jax.ShapeDtypeStruct((3456, 384), F32),
+        ),
+        in_specs=[blocks(2560), blocks(1152), blocks(3456)],
+        out_specs=(blocks(2560), blocks(1152), blocks(3456)),
+        compiler_params=pltpu.CompilerParams(vmem_limit_bytes=40 * 2**20),
+    )(latent_grad.reshape(2560, 384), temporal.reshape(1152, 384), spatial.reshape(3456, 384))
+    return latent_grad.reshape(2, 2, 640, 384), temporal.reshape(3, 384, 384), spatial.reshape(3, 3, 384, 384)
 
 
 def on_device(latents, cotangent, temporal_weight, spatial_weight):
@@ -525,15 +651,17 @@
             pltpu.SemaphoreType.DMA((4,)),
             pltpu.SemaphoreType.DMA((12,)),
             pltpu.SemaphoreType.DMA((CHUNKS, 2)),
-            pltpu.SemaphoreType.DMA((CHUNKS, 2)),
-            pltpu.SemaphoreType.DMA((CHUNKS, 2)),
+            pltpu.SemaphoreType.DMA((CHUNKS, 2, 2)),
+            pltpu.SemaphoreType.DMA((CHUNKS, 2, 2)),
             pltpu.SemaphoreType.DMA((CHUNKS, 2)),
             pltpu.SemaphoreType.DMA((8,)),
+            pltpu.VMEM((2, 2, 176, 384), BF),
+            pltpu.SemaphoreType.DMA((2, 2, 2)),
         ] + Reduce.SCRATCH,
         compiler_params=pltpu.CompilerParams(
             collective_id=0, has_side_effects=True, vmem_limit_bytes=60 * 2**20),
     )(latents, cotangent, temporal_weight, spatial_weight)
-    return (latent_grad, temporal.astype(F32) * scale, spatial.astype(F32) * scale)
+    return scaled(latent_grad, temporal, spatial, scale)
 
 
 def solution(mesh):

time: 115 us -> 95.9 us (0.83)
  Pallas kernels: 106 us -> 90.6 us
  other arithmetic: 6.07 us -> 0 us
  local copies, waits for them, and re-layouts: 2.09 us -> 4.45 us
    pallas_call x1, Pallas kernels: 106 us -> 86.8 us  [on_device(): pl.pallas_call(block_kernel, out_shape=(jax.ShapeDtypeStruct((2, 2, 640,...]
    mul x2 -> x0, other arithmetic: 6.07 us -> none  [the longest x1 4.7 us: on_device(): spatial.astype(F32) * scale]
    pallas_call x0 -> x1, Pallas kernels: none -> 3.76 us  [scaled(): pl.pallas_call(functools.partial(scale_kernel, scale), grid=(4,), out_sha...]
    unnamed x5 -> x6, local copies, waits for them, and re-layouts: 2.09 us -> 4.45 us
where the time goes in v3:
time: 95.9 us; the launch traced here: 95.7 us
  Pallas kernels  90.6 us (94%)
  local copies, waits for them, and re-layouts  4.45 us (5%)
    pallas_call x1, Pallas kernels, on_device(): pl.pallas_call(block_kernel, out_shape=(jax.ShapeDtypeStruct((2, 2, 640,...  86.8 us
    unnamed x6, local copies, waits for them, and re-layouts  4.45 us
    pallas_call x1, Pallas kernels, scaled(): pl.pallas_call(functools.partial(scale_kernel, scale), grid=(4,), out_sha...  3.76 us

profile of v3, /device:TPU:1, one launch (start us, length us, event | category | flops | bytes accessed | tf_op | source)
XLA Modules:
  0.0 95.7 jit_solution(14870938290105477442)
XLA Ops:
  0.6 86.8 %shard_map.67 = (bf16[2,2,640,384]{3,2,1,0:T(8,128)(2,1)}, bf16[3,384,384]{2,1,0:T(8,128)(2,1)}, bf16[3,3,384,384]{3,2,1,0:T(8,128)(2,1)}) custom-call(bf16[2,2,640,384]{3,2,1,0:T(8,128)(2,1)} %lat_hbm.1, bf16[2,2,640,384]{3,2,1,0:T(8,128)(2,1)} %cot_hbm.1, bf16[3,384,384]{2,1,0:T(8,128)(2,1)} %tw_hbm.1, bf16[3,3,384,384]{3,2,1,0:T(8,128)(2,1)} %sw_hbm.1), custom_call_target="tpu_custom_call" | custom-call | tf_op jit(solution)/shard_map/pallas_call | solution.py:630
  87.5 0.0 copy-start
  87.5 1.7 %copy-done = bf16[3,3,384,384]{3,2,1,0:T(8,128)(2,1)S(1)} copy-done((bf16[3,3,384,384]{3,2,1,0:T(8,128)(2,1)S(1)}, bf16[3,3,384,384]{3,2,1,0:T(8,128)(2,1)}, u32[]{:S(2)}) %copy-start) | copy-done | bytes 2654232
  89.2 0.0 copy-start.1
  89.2 1.5 %copy-done.1 = bf16[2,2,640,384]{3,2,1,0:T(8,128)(2,1)S(1)} copy-done((bf16[2,2,640,384]{3,2,1,0:T(8,128)(2,1)S(1)}, bf16[2,2,640,384]{3,2,1,0:T(8,128)(2,1)}, u32[]{:S(2)}) %copy-start.1) | copy-done | bytes 1966104
  90.8 0.0 copy-start.2
  90.8 1.2 %copy-done.2 = bf16[3,384,384]{2,1,0:T(8,128)(2,1)S(1)} copy-done((bf16[3,384,384]{2,1,0:T(8,128)(2,1)S(1)}, bf16[3,384,384]{2,1,0:T(8,128)(2,1)}, u32[]{:S(2)}) %copy-start.2) | copy-done | bytes 884760
  91.9 3.8 %shard_map.68 = (bf16[2560,384]{1,0:T(8,128)(2,1)}, f32[1152,384]{1,0:T(8,128)}, f32[3456,384]{1,0:T(8,128)}) custom-call(bf16[2560,384]{1,0:T(8,128)(2,1)S(1)} %bitcast.7, bf16[1152,384]{1,0:T(8,128)(2,1)S(1)} %bitcast.8, bf16[3456,384]{1,0:T(8,128)(2,1)S(1)} %bitcast.6), custom_call_target="tpu_custom_call" | custom-call | tf_op jit(solution)/shard_map/pallas_call | solution.py:610
Async XLA Ops:
  87.5 1.8 %copy-start = (bf16[3,3,384,384]{3,2,1,0:T(8,128)(2,1)S(1)}, bf16[3,3,384,384]{3,2,1,0:T(8,128)(2,1)}, u32[]{:S(2)}) copy-start(bf16[3,3,384,384]{3,2,1,0:T(8,128)(2,1)} %get-tuple-element.11) | copy-start | bytes 7962628
  89.2 1.5 %copy-start.1 = (bf16[2,2,640,384]{3,2,1,0:T(8,128)(2,1)S(1)}, bf16[2,2,640,384]{3,2,1,0:T(8,128)(2,1)}, u32[]{:S(2)}) copy-start(bf16[2,2,640,384]{3,2,1,0:T(8,128)(2,1)} %get-tuple-element.9) | copy-start | bytes 5898244
  90.8 1.2 %copy-start.2 = (bf16[3,384,384]{2,1,0:T(8,128)(2,1)S(1)}, bf16[3,384,384]{2,1,0:T(8,128)(2,1)}, u32[]{:S(2)}) copy-start(bf16[3,384,384]{2,1,0:T(8,128)(2,1)} %get-tuple-element.10) | copy-start | bytes 2654212

commit v4 on v3

--- a/solution.py
+++ b/solution.py
@@ -363,9 +363,9 @@
                     to_mirror(way, c, f).wait_recv()
                     (to_band if c == 1 else to_mirror)(way, c, f).start()
 
-    def forward_second(f):
+    def forward_second(f, chunks):
         for way in range(2):
-            for c in (0, 2, 3):
+            for c in chunks:
                 @pl.when(here(way, c) & (place.half == 1 - way))
                 def _():
                     to_mirror(way, c, f).wait_recv()
@@ -383,10 +383,15 @@
                 def _():
                     to_mirror(way, c, f).wait_send()
 
-    def p_copy(c):
+    def p_copy(c, f):
         cols = pl.ds(c * CW, CW)
-        return remote(pgx.at[0:2, :, cols], pgx.at[2:4, :, cols], p_sem.at[c, 0], p_sem.at[c, 1],
+        return remote(pgx.at[f, :, cols], pgx.at[f + 2, :, cols], p_sem.at[c, f, 0], p_sem.at[c, f, 1],
                       ((tm + 3) % 4, height))
+
+    def give(c, f):
+        @pl.when(tm > 0)
+        def _():
+            p_copy(c, f).start()
 
     for c in range(CHUNKS):
         for f in range(2):
@@ -437,7 +442,6 @@
         back[0, f] = nt(lanes(cot3[1, f], cot3[2, f]), lanes(sw[1], sw[0]))
         forward_first(f)
         back[1, f] = nt(lanes(cot3[2, f], cot3[1, f]), lanes(sw[1], sw[2]))
-    forward_second(0)
     lat_in.wait()
     tw_in.wait()
     for copy in twt_in:
@@ -459,10 +463,8 @@
             add(3, slice(k * 384, (k + 1) * 384), half, value)
 
     weight = tw.reshape(1152, 384)
-    for c in range(CHUNKS):
+    def forward_part(c):
         cols = slice(c * CW, (c + 1) * CW)
-        if c == 1:
-            forward_second(1)
 
         @pl.when(tm > 0)
         def _():
@@ -478,6 +480,10 @@
             for f in range(2):
                 hid[r, f, cols] = hidden[f * CW:(f + 1) * CW]
             factors.append(sigma * (1.0 + pre * (1.0 - sigma)))
+        return factors
+
+    def backward_part(c, factors):
+        cols = slice(c * CW, (c + 1) * CW)
         for f in range(2):
             @pl.when(height > 0)
             def _():
@@ -498,16 +504,22 @@
             for f in range(2):
                 pgx[f, r, cols] = grad[f * CW:(f + 1) * CW]
 
-        @pl.when(tm > 0)
-        def _():
-            p_copy(c).start()
-
-        if c == 1:
-            for i in range(3):
-                spatial(i, 0)
-            temporal(0)
+        for f in range(2):
+            give(c, f)
 
     red = Reduce(place, part, out, refs)
+    backward_part(0, forward_part(0))
+    forward_second(0, (0,))
+    backward_part(1, forward_part(1))
+    forward_second(1, (0,))
+    forward_second(0, (2, 3))
+    spatial(0, 0)
+    spatial(1, 0)
+    forward_second(1, (2, 3))
+    backward_part(2, forward_part(2))
+    spatial(2, 0)
+    temporal(0)
+    backward_part(3, forward_part(3))
 
     def latent(f, r):
         grads = lanes(*(pgx[f + k, r] for k in range(3)))
@@ -520,22 +532,23 @@
 
     def arrive():
         for c in range(CHUNKS):
-            @pl.when(tm < 3)
-            def _():
-                p_copy(c).wait_recv()
+            for f in range(2):
+                @pl.when(tm < 3)
+                def _():
+                    p_copy(c, f).wait_recv()
 
     def last(g):
         red.step7(g)
         store(g).start()
 
+    spatial(1, 1)
+    red.step0(1)
     spatial(0, 1)
+    red.step1(1)
     red.step0(0)
-    spatial(1, 1)
+    spatial(2, 1)
+    red.step0(2)
     red.step1(0)
-    red.step0(1)
-    spatial(2, 1)
-    red.step1(1)
-    red.step0(2)
     temporal(1)
     red.step1(2)
     red.step0(3)
@@ -543,28 +556,28 @@
     red.step2(1)
     red.step1(3)
     red.step2(2)
-    arrive()
-    latent(0, 0)
     red.step2(3)
-    latent(0, 1)
     red.step3(0)
     red.step3(1)
     red.step3(2)
     red.step3(3)
-    latent(1, 0)
     red.step4(0)
     red.step4(1)
     red.step4(2)
     red.step4(3)
-    latent(1, 1)
     red.step5(0)
     red.step5(1)
     red.step5(2)
     red.step5(3)
+    arrive()
+    latent(0, 0)
+    latent(0, 1)
+    latent(1, 0)
     red.step6(0)
     red.step6(1)
     red.step6(2)
     red.step6(3)
+    latent(1, 1)
     last(0)
     last(1)
     last(2)
@@ -584,9 +597,9 @@
             def _():
                 up_copy(c, f).wait_send()
 
-        @pl.when(tm > 0)
-        def _():
-            p_copy(c).wait_send()
+            @pl.when(tm > 0)
+            def _():
+                p_copy(c, f).wait_send()
     for f in range(2):
         forward_sends(f)
     for g in range(4):
@@ -617,7 +630,7 @@
         ),
         in_specs=[blocks(2560), blocks(1152), blocks(3456)],
         out_specs=(blocks(2560), blocks(1152), blocks(3456)),
-        compiler_params=pltpu.CompilerParams(vmem_limit_bytes=40 * 2**20),
+        compiler_params=pltpu.CompilerParams(vmem_limit_bytes=60 * 2**20),
     )(latent_grad.reshape(2560, 384), temporal.reshape(1152, 384), spatial.reshape(3456, 384))
     return latent_grad.reshape(2, 2, 640, 384), temporal.reshape(3, 384, 384), spatial.reshape(3, 3, 384, 384)
 
@@ -653,7 +666,7 @@
             pltpu.SemaphoreType.DMA((CHUNKS, 2)),
             pltpu.SemaphoreType.DMA((CHUNKS, 2, 2)),
             pltpu.SemaphoreType.DMA((CHUNKS, 2, 2)),
-            pltpu.SemaphoreType.DMA((CHUNKS, 2)),
+            pltpu.SemaphoreType.DMA((CHUNKS, 2, 2)),
             pltpu.SemaphoreType.DMA((8,)),
             pltpu.VMEM((2, 2, 176, 384), BF),
             pltpu.SemaphoreType.DMA((2, 2, 2)),

time: 95.9 us -> 96.3 us (level)
  Pallas kernels: 90.6 us -> 95.4 us
  local copies, waits for them, and re-layouts: 4.45 us -> 0 us
    unnamed x6 -> x0, local copies, waits for them, and re-layouts: 4.45 us -> none
    pallas_call x1, Pallas kernels: 3.76 us -> 6.46 us  [scaled(): pl.pallas_call(functools.partial(scale_kernel, scale), grid=(4,), out_sha...]
    pallas_call x1, Pallas kernels: 86.8 us -> 89 us  [on_device(): pl.pallas_call(block_kernel, out_shape=(jax.ShapeDtypeStruct((2, 2, 640,...]
where the time goes in v4:
time: 96.3 us; the launch traced here: 96.1 us
  Pallas kernels  95.4 us (99%)
    pallas_call x1, Pallas kernels, on_device(): pl.pallas_call(block_kernel, out_shape=(jax.ShapeDtypeStruct((2, 2, 640,...  89 us
    pallas_call x1, Pallas kernels, scaled(): pl.pallas_call(functools.partial(scale_kernel, scale), grid=(4,), out_sha...  6.46 us

profile of v4, /device:TPU:1, one launch (start us, length us, event | category | flops | bytes accessed | tf_op | source)
XLA Modules:
  0.0 96.1 jit_solution(14889701469448586002)
XLA Ops:
  0.6 89.0 %shard_map.67 = (bf16[2,2,640,384]{3,2,1,0:T(8,128)(2,1)}, bf16[3,384,384]{2,1,0:T(8,128)(2,1)}, bf16[3,3,384,384]{3,2,1,0:T(8,128)(2,1)}) custom-call(bf16[2,2,640,384]{3,2,1,0:T(8,128)(2,1)} %lat_hbm.1, bf16[2,2,640,384]{3,2,1,0:T(8,128)(2,1)} %cot_hbm.1, bf16[3,384,384]{2,1,0:T(8,128)(2,1)} %tw_hbm.1, bf16[3,3,384,384]{3,2,1,0:T(8,128)(2,1)} %sw_hbm.1), custom_call_target="tpu_custom_call" | custom-call | tf_op jit(solution)/shard_map/pallas_call | solution.py:643
  89.6 6.5 %shard_map.68 = (bf16[2560,384]{1,0:T(8,128)(2,1)}, f32[1152,384]{1,0:T(8,128)}, f32[3456,384]{1,0:T(8,128)}) custom-call(bf16[2560,384]{1,0:T(8,128)(2,1)} %bitcast.7, bf16[1152,384]{1,0:T(8,128)(2,1)} %bitcast.8, bf16[3456,384]{1,0:T(8,128)(2,1)} %bitcast.6), custom_call_target="tpu_custom_call" | custom-call | tf_op jit(solution)/shard_map/pallas_call | solution.py:623

commit v5 on v3

--- a/solution.py
+++ b/solution.py
@@ -459,10 +459,8 @@
             add(3, slice(k * 384, (k + 1) * 384), half, value)
 
     weight = tw.reshape(1152, 384)
-    for c in range(CHUNKS):
+    def forward_part(c):
         cols = slice(c * CW, (c + 1) * CW)
-        if c == 1:
-            forward_second(1)
 
         @pl.when(tm > 0)
         def _():
@@ -478,6 +476,10 @@
             for f in range(2):
                 hid[r, f, cols] = hidden[f * CW:(f + 1) * CW]
             factors.append(sigma * (1.0 + pre * (1.0 - sigma)))
+        return factors
+
+    def backward_part(c, factors):
+        cols = slice(c * CW, (c + 1) * CW)
         for f in range(2):
             @pl.when(height > 0)
             def _():
@@ -502,12 +504,18 @@
         def _():
             p_copy(c).start()
 
-        if c == 1:
-            for i in range(3):
-                spatial(i, 0)
-            temporal(0)
-
     red = Reduce(place, part, out, refs)
+    backward_part(0, forward_part(0))
+    forward_second(1)
+    backward_part(1, forward_part(1))
+    for i in range(3):
+        spatial(i, 0)
+    temporal(0)
+    factors = [forward_part(c) for c in (2, 3)]
+    spatial(1, 1)
+    red.step0(1)
+    for c in (2, 3):
+        backward_part(c, factors[c - 2])
 
     def latent(f, r):
         grads = lanes(*(pgx[f + k, r] for k in range(3)))
@@ -530,12 +538,10 @@
 
     spatial(0, 1)
     red.step0(0)
-    spatial(1, 1)
+    red.step1(1)
+    spatial(2, 1)
+    red.step0(2)
     red.step1(0)
-    red.step0(1)
-    spatial(2, 1)
-    red.step1(1)
-    red.step0(2)
     temporal(1)
     red.step1(2)
     red.step0(3)
@@ -543,28 +549,28 @@
     red.step2(1)
     red.step1(3)
     red.step2(2)
-    arrive()
-    latent(0, 0)
     red.step2(3)
-    latent(0, 1)
     red.step3(0)
     red.step3(1)
     red.step3(2)
     red.step3(3)
-    latent(1, 0)
     red.step4(0)
     red.step4(1)
     red.step4(2)
     red.step4(3)
-    latent(1, 1)
     red.step5(0)
     red.step5(1)
     red.step5(2)
     red.step5(3)
+    arrive()
+    latent(0, 0)
+    latent(0, 1)
+    latent(1, 0)
     red.step6(0)
     red.step6(1)
     red.step6(2)
     red.step6(3)
+    latent(1, 1)
     last(0)
     last(1)
     last(2)
@@ -617,7 +623,7 @@
         ),
         in_specs=[blocks(2560), blocks(1152), blocks(3456)],
         out_specs=(blocks(2560), blocks(1152), blocks(3456)),
-        compiler_params=pltpu.CompilerParams(vmem_limit_bytes=40 * 2**20),
+        compiler_params=pltpu.CompilerParams(vmem_limit_bytes=60 * 2**20),
     )(latent_grad.reshape(2560, 384), temporal.reshape(1152, 384), spatial.reshape(3456, 384))
     return latent_grad.reshape(2, 2, 640, 384), temporal.reshape(3, 384, 384), spatial.reshape(3, 3, 384, 384)
 

time: 95.9 us -> 94.2 us (0.982)
  local copies, waits for them, and re-layouts: 4.45 us -> 0 us
  Pallas kernels: 90.6 us -> 93.3 us
    unnamed x6 -> x0, local copies, waits for them, and re-layouts: 4.45 us -> none
    pallas_call x1, Pallas kernels: 3.76 us -> 6.46 us  [scaled(): pl.pallas_call(functools.partial(scale_kernel, scale), grid=(4,), out_sha...]
where the time goes in v5:
time: 94.2 us; the launch traced here: 94 us
  Pallas kernels  93.3 us (99%)
    pallas_call x1, Pallas kernels, on_device(): pl.pallas_call(block_kernel, out_shape=(jax.ShapeDtypeStruct((2, 2, 640,...  86.9 us
    pallas_call x1, Pallas kernels, scaled(): pl.pallas_call(functools.partial(scale_kernel, scale), grid=(4,), out_sha...  6.46 us

profile of v5, /device:TPU:1, one launch (start us, length us, event | category | flops | bytes accessed | tf_op | source)
XLA Modules:
  0.0 94.0 jit_solution(11885936927145798748)
XLA Ops:
  0.6 86.9 %shard_map.67 = (bf16[2,2,640,384]{3,2,1,0:T(8,128)(2,1)}, bf16[3,384,384]{2,1,0:T(8,128)(2,1)}, bf16[3,3,384,384]{3,2,1,0:T(8,128)(2,1)}) custom-call(bf16[2,2,640,384]{3,2,1,0:T(8,128)(2,1)} %lat_hbm.1, bf16[2,2,640,384]{3,2,1,0:T(8,128)(2,1)} %cot_hbm.1, bf16[3,384,384]{2,1,0:T(8,128)(2,1)} %tw_hbm.1, bf16[3,3,384,384]{3,2,1,0:T(8,128)(2,1)} %sw_hbm.1), custom_call_target="tpu_custom_call" | custom-call | tf_op jit(solution)/shard_map/pallas_call | solution.py:636
  87.5 6.5 %shard_map.68 = (bf16[2560,384]{1,0:T(8,128)(2,1)}, f32[1152,384]{1,0:T(8,128)}, f32[3456,384]{1,0:T(8,128)}) custom-call(bf16[2560,384]{1,0:T(8,128)(2,1)} %bitcast.7, bf16[1152,384]{1,0:T(8,128)(2,1)} %bitcast.8, bf16[3456,384]{1,0:T(8,128)(2,1)} %bitcast.6), custom_call_target="tpu_custom_call" | custom-call | tf_op jit(solution)/shard_map/pallas_call | solution.py:616

commit v6 on v5

--- a/solution.py
+++ b/solution.py
@@ -437,7 +437,6 @@
         back[0, f] = nt(lanes(cot3[1, f], cot3[2, f]), lanes(sw[1], sw[0]))
         forward_first(f)
         back[1, f] = nt(lanes(cot3[2, f], cot3[1, f]), lanes(sw[1], sw[2]))
-    forward_second(0)
     lat_in.wait()
     tw_in.wait()
     for copy in twt_in:
@@ -505,11 +504,15 @@
             p_copy(c).start()
 
     red = Reduce(place, part, out, refs)
-    backward_part(0, forward_part(0))
+    factors = [forward_part(0)]
+    forward_second(0)
+    factors.append(forward_part(1))
+    spatial(1, 0)
     forward_second(1)
-    backward_part(1, forward_part(1))
-    for i in range(3):
-        spatial(i, 0)
+    for c in (0, 1):
+        backward_part(c, factors[c])
+    spatial(0, 0)
+    spatial(2, 0)
     temporal(0)
     factors = [forward_part(c) for c in (2, 3)]
     spatial(1, 1)
@@ -611,11 +614,11 @@
 
 def scaled(latent_grad, temporal, spatial, scale):
     def blocks(rows):
-        return pl.BlockSpec((rows // 4, 384), lambda i: (i, 0))
+        return pl.BlockSpec((rows // 8, 384), lambda i: (i, 0))
 
     latent_grad, temporal, spatial = pl.pallas_call(
         functools.partial(scale_kernel, scale),
-        grid=(4,),
+        grid=(8,),
         out_shape=(
             jax.ShapeDtypeStruct((2560, 384), BF),
             jax.ShapeDtypeStruct((1152, 384), F32),

time: 94.2 us -> 98.8 us (1.049)
  Pallas kernels: 93.3 us -> 97.9 us
    pallas_call x1, Pallas kernels: 86.9 us -> 89.7 us  [on_device(): pl.pallas_call(block_kernel, out_shape=(jax.ShapeDtypeStruct((2, 2, 640,...]
    pallas_call x1, Pallas kernels: 6.46 us -> 8.16 us  [scaled(): pl.pallas_call(functools.partial(scale_kernel, scale), grid=(8,), out_sha...]
where the time goes in v6:
time: 98.8 us; the launch traced here: 98.5 us
  Pallas kernels  97.9 us (99%)
    pallas_call x1, Pallas kernels, on_device(): pl.pallas_call(block_kernel, out_shape=(jax.ShapeDtypeStruct((2, 2, 640,...  89.7 us
    pallas_call x1, Pallas kernels, scaled(): pl.pallas_call(functools.partial(scale_kernel, scale), grid=(8,), out_sha...  8.16 us

profile of v6, /device:TPU:1, one launch (start us, length us, event | category | flops | bytes accessed | tf_op | source)
XLA Modules:
  0.0 98.5 jit_solution(8937603143158345299)
XLA Ops:
  0.6 89.7 %shard_map.67 = (bf16[2,2,640,384]{3,2,1,0:T(8,128)(2,1)}, bf16[3,384,384]{2,1,0:T(8,128)(2,1)}, bf16[3,3,384,384]{3,2,1,0:T(8,128)(2,1)}) custom-call(bf16[2,2,640,384]{3,2,1,0:T(8,128)(2,1)} %lat_hbm.1, bf16[2,2,640,384]{3,2,1,0:T(8,128)(2,1)} %cot_hbm.1, bf16[3,384,384]{2,1,0:T(8,128)(2,1)} %tw_hbm.1, bf16[3,3,384,384]{3,2,1,0:T(8,128)(2,1)} %sw_hbm.1), custom_call_target="tpu_custom_call" | custom-call | tf_op jit(solution)/shard_map/pallas_call | solution.py:639
  90.3 8.2 %shard_map.68 = (bf16[2560,384]{1,0:T(8,128)(2,1)}, f32[1152,384]{1,0:T(8,128)}, f32[3456,384]{1,0:T(8,128)}) custom-call(bf16[2560,384]{1,0:T(8,128)(2,1)} %bitcast.7, bf16[1152,384]{1,0:T(8,128)(2,1)} %bitcast.8, bf16[3456,384]{1,0:T(8,128)(2,1)} %bitcast.6), custom_call_target="tpu_custom_call" | custom-call | tf_op jit(solution)/shard_map/pallas_call | solution.py:619
